TPU v7x, 128 devices: a whole 4x4x4 slice. The times are simulated.
128 devices in a mesh: dp: 16 (over z_hi, x, core), tensor: 8 (over y, z_lo).
Axes of the slice: x: 4, y: 4, z: 4 (z_hi: 2, z_lo: 2; z = z_hi * 2 + z_lo), core: 2. Of those that a mesh axis runs over, the one named last changes fastest.
Arguments:
- partial_grads: bfloat16 [16, 1024, 28672], P('dp', None, 'tensor'), may hold values from -6 to 6
- master: float32 [1024, 28672], P(('dp', 'tensor')), may hold values from -6 to 6
- first_moment: float32 [1024, 28672], P(('dp', 'tensor')), may hold values from -6 to 6
- second_moment: float32 [1024, 28672], P(('dp', 'tensor')), may hold values from 0.01 to 4
- noise_draws: bfloat16 [16, 1024, 28672], P(None, ('dp', 'tensor')), may hold values from -6 to 6
- band_coeffs: int32 [16], replicated, may hold values from 1 to 32
- step: int32 [1], replicated, may hold values from 0 to 15
Outputs:
- new_master: float32 [1024, 28672], P(('dp', 'tensor'))
- new_first: float32 [1024, 28672], P(('dp', 'tensor'))
- new_second: float32 [1024, 28672], P(('dp', 'tensor'))
- weights: bfloat16 [1024, 28672], P(None, 'tensor')
All inputs are finite; a program needn't handle non-finite values.
Results may differ from a plain program's by a relative error of at most 0.0035.
Values may be sent and summed in bfloat16 or wider, within the bound.
No kernel may reach another device: no remote copies, remote signals or barrier semaphores. Data moves between devices by JAX's collectives and lax.ppermute only.
A program may use at most 128 MiB of HBM per device.

v0:
```python
import jax
import jax.numpy as jnp
from jax import lax
from jax.sharding import PartitionSpec as P

HISTORY = 16


def local(partial_grads, master, first_moment, second_moment, noise_draws, band_coeffs, step):
    own_part = partial_grads[0]
    summed = lax.psum_scatter(
        own_part.astype(jnp.float32).astype(jnp.bfloat16), "dp", scatter_dimension=0, tiled=True
    ).astype(jnp.float32)
    grad_sum = lax.all_to_all(
        summed.astype(jnp.bfloat16), "tensor", split_axis=0, concat_axis=1, tiled=True
    ).astype(summed.dtype)
    slots = jnp.arange(HISTORY, dtype=jnp.int32)
    lags = (step[0] - slots) % HISTORY
    onehot = (lags[:, None] == slots[None, :]).astype(jnp.float32)
    slot_weight = jnp.sum(onehot * band_coeffs[None, :].astype(jnp.float32), axis=1) / 32.0
    noise = jnp.einsum(
        "s,srf->rf",
        slot_weight.astype(jnp.bfloat16),
        noise_draws,
        preferred_element_type=jnp.float32,
    )
    gradient = 0.25 * (grad_sum + noise)
    new_first = 0.9 * first_moment + 0.1 * gradient
    new_second = 0.95 * second_moment + 0.05 * gradient * gradient
    count = (step[0] + 1).astype(jnp.float32)
    correct_one = 1.0 - jnp.power(jnp.float32(0.9), count)
    correct_two = 1.0 - jnp.power(jnp.float32(0.95), count)
    update = new_first / correct_one / (jnp.sqrt(new_second / correct_two) + 1e-08) + 0.1 * master
    new_master = master - 0.02 * update
    rounded = new_master.astype(jnp.bfloat16)
    columns = lax.all_to_all(rounded, "tensor", split_axis=1, concat_axis=0, tiled=True)
    weights = lax.all_gather(columns, "dp", axis=0, tiled=True)
    return (new_master, new_first, new_second, weights)


def solution(mesh):
    placed = (
        P("dp", None, "tensor"),
        P(("dp", "tensor"), None),
        P(("dp", "tensor"), None),
        P(("dp", "tensor"), None),
        P(None, ("dp", "tensor"), None),
        P(),
        P(),
    )
    return jax.shard_map(
        local,
        mesh=mesh,
        in_specs=placed,
        out_specs=(
            P(("dp", "tensor"), None),
            P(("dp", "tensor"), None),
            P(("dp", "tensor"), None),
            P(None, "tensor"),
        ),
        check_vma=False,
    )
```

profile of v0, /device:TPU:1, one launch (start us, length us, event | category | flops | bytes accessed | tf_op | source)
XLA Modules:
  0.0 223.4 jit_solution(17266211974802031157)
XLA Ops:
  7.2 0.0 copy-start.2
  7.2 0.0 reduce-scatter.2.cloned.1.call-start
  7.2 0.0 copy-start
  7.2 0.0 copy-start.1
  7.2 0.7 reduce-scatter.2.cloned.1.call-update
  8.6 0.0 copy-done.2
  8.7 0.2 select_reduce_fusion
  8.9 99.4 %reduce-scatter.2.cloned.1.call-done = bf16[64,3584]{1,0:T(8,128)(2,1)} async-done(((bf16[1024,3584]{1,0:T(8,128)(2,1)}), bf16[64,3584]{1,0:T(8,128)(2,1)}) %reduce-scatter.2.cloned.1.call-update) | async-done | bytes 458768 | tf_op jit(solution)/shard_map/reduce_scatter | solution.py:11
  108.3 4.1 %all-to-all-start = ((bf16[8,8,3584]{2,1,0:T(8,128)(2,1)}), bf16[8,8,3584]{2,1,0:T(8,128)(2,1)S(1)}, u32[]{:S(2)}, u32[]{:S(2)}) async-start(bf16[8,8,3584]{2,1,0:T(8,128)(2,1)} %bitcast.27), calls=%async_computation.1 | async-start | bytes 917504 | tf_op jit(solution)/shard_map/all_to_all | solution.py:14
  112.4 0.0 all-gather.2.cloned.1.call-start
  112.5 11.3 %fusion = f32[1,8,28672]{2,0,1:T(1,128)S(1)} fusion(bf16[16,8,28672]{2,1,0:T(8,128)(2,1)} %param.11, f32[16]{0:T(128)S(1)} %select_reduce_fusion), kind=kOutput, calls=%fused_computation | convolution fusion | flops 7340064 | bytes 8257600 | tf_op jit(solution)/shard_map/s,srf->rf/dot_general | solution.py:21
  123.8 0.0 all-to-all-done
  123.8 0.1 convert_element_type.35
  123.8 0.0 copy-done
  123.8 0.0 copy-done.1
  123.8 3.7 %fusion.8 = (bf16[8,28672]{1,0:T(8,128)(2,1)S(1)}, f32[8,28672]{1,0:T(8,128)}, f32[8,28672]{1,0:T(8,128)}, f32[8,28672]{1,0:T(8,128)}) fusion(f32[8,28672]{1,0:T(8,128)S(1)} %copy-done, f32[]{:T(128)S(6)} %sub.22, f32[]{:T(128)S(6)} %sub.21, f32[8,28672]{1,0:T(8,128)S(1)} %bitcast.24, f32[1,8,28672]{2,0,1:T(1,128)S(1)} %fusion, f32[8,28672]{1,0:T(8,128)S(1)} %copy-done.1, ...), kind=kLoop, calls=%fused_computation.17 | loop fusion | flops 4128768 | bytes 7798792 | tf_op jit(solution)/shard_map/convert_element_type | solution.py:35
  127.6 12.0 %all_to_all.32 = bf16[8,8,3584]{2,0,1:T(8,128)(2,1)} all-to-all(bf16[8,8,3584]{2,0,1:T(8,128)(2,1)S(1)} %bitcast.26), channel_id=1, replica_groups=mesh['dp'=16,'tensor'=8] {'tensor'}, dimensions={1} | all-to-all | bytes 917504 | tf_op jit(solution)/shard_map/all_to_all | solution.py:36
  139.5 0.0 all-gather.2.cloned.1.call-update
  139.6 70.4 %all-gather.2.cloned.1.call-done = bf16[1024,3584]{1,0:T(8,128)(2,1)} async-done(((bf16[64,3584]{1,0:T(8,128)(2,1)}), bf16[1024,3584]{1,0:T(8,128)(2,1)}) %all-gather.2.cloned.1.call-update) | async-done | bytes 7340048 | tf_op jit(solution)/shard_map/all_gather | solution.py:37
  209.9 6.6 %copy.24 = bf16[1024,3584]{1,0:T(8,128)(2,1)} copy(bf16[1024,3584]{1,0:T(8,128)(2,1)} %all-gather.2.cloned.1.call-done) | data formatting | bytes 14680064
  (2 shorter events, 0.0 us)
Async XLA Ops:
  7.2 1.5 copy-start.2
  7.2 101.1 %reduce-scatter.2.cloned.1.call-start = ((), (), s32[]{:S(2)}) async-start(), calls=%async_computation.3 | async-start | bytes 7798784 | tf_op jit(solution)/shard_map/reduce_scatter | solution.py:11
  7.2 116.6 %copy-start = (f32[8,28672]{1,0:T(8,128)S(1)}, f32[8,28672]{1,0:T(8,128)}, u32[]{:S(2)}) copy-start(f32[8,28672]{1,0:T(8,128)} %param.8) | copy-start | bytes 2752516
  7.2 116.6 %copy-start.1 = (f32[8,28672]{1,0:T(8,128)S(1)}, f32[8,28672]{1,0:T(8,128)}, u32[]{:S(2)}) copy-start(f32[8,28672]{1,0:T(8,128)} %param.10) | copy-start | bytes 2752516
  108.3 15.5 %all-to-all-start = ((bf16[8,8,3584]{2,1,0:T(8,128)(2,1)}), bf16[8,8,3584]{2,1,0:T(8,128)(2,1)S(1)}, u32[]{:S(2)}, u32[]{:S(2)}) async-start(bf16[8,8,3584]{2,1,0:T(8,128)(2,1)} %bitcast.27), calls=%async_computation.1 | async-start | bytes 917504 | tf_op jit(solution)/shard_map/all_to_all | solution.py:14
  112.4 97.5 %all-gather.2.cloned.1.call-start = ((), (), s32[]{:S(2)}) async-start(), calls=%async_computation.4 | async-start | bytes 7798784 | tf_op jit(solution)/shard_map/all_gather | solution.py:37
Sparse Core Ops, SparseCore 0:
  12.2 96.0 reduce-scatter.1
  139.7 70.2 all-gather.1
where the time goes:
time: 224 us; the launch traced here: 223 us
  waiting for transfers between devices  170 us (76%)
  between operations  14.8 us (7%)
  blocking collectives  12 us (5%)
  matrix products  11.3 us (5%)
  local copies, waits for them, and re-layouts  6.61 us (3%)
  starting transfers between devices  4.21 us (2%)
  other arithmetic  3.98 us (2%)
    reduce_scatter x1, waiting for transfers between devices, local(): lax.psum_scatter(own_part.astype(jnp.float32).astype(jnp.bfloat16), 'dp',...  99.4 us
    all_gather x1, waiting for transfers between devices, local(): weights = lax.all_gather(columns, 'dp', axis=0, tiled=True)  70.4 us
    all_to_all x1, blocking collectives, local(): lax.all_to_all(rounded, 'tensor', split_axis=1, concat_axis=0, tiled=True)  12 us
    dot_general x1, matrix products, local(): jnp.einsum('s,srf->rf', slot_weight.astype(jnp.bfloat16), noise_draws, pr...  11.3 us
    unnamed x7, local copies, waits for them, and re-layouts  6.61 us
  transfers between devices with their start and end apart: 3, of which 2 were waited for; matrix products, arithmetic and copies ran while one was open for 5% of the time, Pallas kernels for 0%

commit v1 on v0

v1 whole, which is shorter than its diff:
```python
import functools

import jax
import jax.numpy as jnp
from jax import lax
from jax.experimental import pallas as pl
from jax.experimental.pallas import tpu as pltpu
from jax.sharding import Mesh, PartitionSpec as P

HISTORY = 16
GROUP = ("z_hi", "x", "y", "z_lo")
DP = ("z_hi", "x", "core")
TENSOR = ("y", "z_lo")
SWAP = [(0, 1), (1, 0)]
VMEM_BYTES = 16 * 1024 * 1024


def noise_kernel(coeffs_ref, step_ref, draws_ref, noise_ref):
    total = None
    for slot in range(HISTORY):
        weight = coeffs_ref[(step_ref[0] - slot) & (HISTORY - 1)].astype(jnp.float32) / 32.0
        term = weight * draws_ref[slot].astype(jnp.float32)
        total = term if total is None else total + term
    noise_ref[...] = total


def noise_sum(band_coeffs, step, noise_draws, parts):
    slots, rows, columns = noise_draws.shape
    width = columns // parts
    return pl.pallas_call(
        noise_kernel,
        out_shape=jax.ShapeDtypeStruct((rows, columns), jnp.float32),
        grid=(parts,),
        in_specs=[
            pl.BlockSpec(memory_space=pltpu.SMEM),
            pl.BlockSpec(memory_space=pltpu.SMEM),
            pl.BlockSpec((slots, rows, width), lambda i: (0, 0, i)),
        ],
        out_specs=pl.BlockSpec((rows, width), lambda i: (0, i)),
        compiler_params=pltpu.CompilerParams(vmem_limit_bytes=VMEM_BYTES),
        cost_estimate=pl.CostEstimate(
            flops=2 * slots * rows * columns, bytes_accessed=2 * slots * rows * columns, transcendentals=0
        ),
        name="noise_sum",
    )(band_coeffs, step, noise_draws)


def adam_kernel(
    correct_ref, sums_ref, noise_ref, master_ref, first_ref, second_ref,
    new_master_ref, new_first_ref, new_second_ref, rounded_ref,
):
    sources, copies = sums_ref.shape[0], rounded_ref.shape[0]
    grad_sum = sums_ref[0, 0].astype(jnp.float32)
    for source in range(1, sources):
        grad_sum = grad_sum + sums_ref[source, 0].astype(jnp.float32)
    gradient = 0.25 * (grad_sum + noise_ref[...])
    new_first = 0.9 * first_ref[...] + 0.1 * gradient
    new_second = 0.95 * second_ref[...] + 0.05 * gradient * gradient
    master = master_ref[...]
    update = new_first / correct_ref[0] / (jnp.sqrt(new_second / correct_ref[1]) + 1e-08) + 0.1 * master
    new_master = master - 0.02 * update
    new_master_ref[...] = new_master
    new_first_ref[...] = new_first
    new_second_ref[...] = new_second
    rounded = new_master.astype(jnp.bfloat16)
    for copy in range(copies):
        rounded_ref[copy, 0] = rounded


def adam(correct, sums, noise, master, first, second):
    sources, parts, rows, width = sums.shape
    state = pl.BlockSpec((rows, width), lambda i: (0, i))
    spread = pl.BlockSpec((sources, 1, rows, width), lambda i: (0, i, 0, 0))
    whole = jax.ShapeDtypeStruct(master.shape, jnp.float32)
    return pl.pallas_call(
        adam_kernel,
        out_shape=(whole, whole, whole, jax.ShapeDtypeStruct(sums.shape, jnp.bfloat16)),
        grid=(parts,),
        in_specs=[pl.BlockSpec(memory_space=pltpu.SMEM), spread, state, state, state, state],
        out_specs=(state, state, state, spread),
        compiler_params=pltpu.CompilerParams(vmem_limit_bytes=VMEM_BYTES),
        name="adam",
    )(correct, sums, noise, master, first, second)


def place_kernel(side_ref, block_ref, *refs):
    out_ref, sem = refs[-2:]
    copy = pltpu.make_async_copy(block_ref, out_ref.at[:, side_ref[0]], sem)
    copy.start()
    copy.wait()


def place(block, side, into=None):
    chips, rows, columns = block.shape
    anywhere = pl.BlockSpec(memory_space=pl.ANY)
    more = () if into is None else (into,)
    return pl.pallas_call(
        place_kernel,
        out_shape=jax.ShapeDtypeStruct((chips, 2, rows, columns), block.dtype),
        in_specs=[pl.BlockSpec(memory_space=pltpu.SMEM), anywhere] + [anywhere] * len(more),
        out_specs=anywhere,
        scratch_shapes=[pltpu.SemaphoreType.DMA],
        input_output_aliases={2: 0} if more else {},
        compiler_params=pltpu.CompilerParams(vmem_limit_bytes=1024 * 1024),
        cost_estimate=pl.CostEstimate(flops=0, bytes_accessed=4 * block.size, transcendentals=0),
        name="place",
    )(side.reshape(1), block, *more)


def local(chips, tensors, partial_grads, master, first_moment, second_moment, noise_draws, band_coeffs, step):
    core = lax.axis_index("core")
    _, rows, width = partial_grads.shape
    own_rows = rows // (2 * chips * tensors)

    halves = partial_grads.reshape(chips, 2, rows // (2 * chips), width)
    given = lax.dynamic_index_in_dim(halves, 1 - core, 1, keepdims=False)
    kept = lax.dynamic_index_in_dim(halves, core, 1, keepdims=False)
    received = lax.ppermute(given, "core", SWAP)
    paired = (kept.astype(jnp.float32) + received.astype(jnp.float32)).astype(jnp.bfloat16)

    pieces = paired.reshape(chips * tensors, own_rows, width)
    sums = lax.all_to_all(pieces, GROUP, split_axis=0, concat_axis=0, tiled=True)
    sums = sums.reshape(chips, tensors, own_rows, width)

    noise = noise_sum(band_coeffs, step, noise_draws, tensors)
    count = (step[0] + 1).astype(jnp.float32)
    correct = 1.0 - jnp.power(jnp.array([0.9, 0.95], jnp.float32), count)
    new_master, new_first, new_second, spread = adam(
        correct, sums, noise, master, first_moment, second_moment
    )

    gathered = lax.all_to_all(
        spread.reshape(chips * tensors, own_rows, width), GROUP, split_axis=0, concat_axis=0, tiled=True
    ).reshape(chips, tensors * own_rows, width)
    other = lax.ppermute(gathered, "core", SWAP)
    weights = place(gathered, core)
    weights = place(other, 1 - core, weights)
    return (new_master, new_first, new_second, weights.reshape(rows, width))


def solution(mesh):
    fine = Mesh(mesh.devices.reshape(2, 4, 2, 4, 2), ("z_hi", "x", "core", "y", "z_lo"))
    owners = DP + TENSOR
    return jax.shard_map(
        functools.partial(local, 8, 8),
        mesh=fine,
        in_specs=(
            P(DP, None, TENSOR),
            P(owners, None),
            P(owners, None),
            P(owners, None),
            P(None, owners, None),
            P(),
            P(),
        ),
        out_specs=(P(owners, None), P(owners, None), P(owners, None), P(None, TENSOR)),
        check_vma=False,
    )
```

time: 224 us -> 148 us (0.66)
  waiting for transfers between devices: 170 us -> 48.7 us
  blocking collectives: 12 us -> 52.8 us
  between operations: 14.8 us -> 1.35 us
  starting transfers between devices: 4.21 us -> 17.4 us
  Pallas kernels: 0 us -> 12.9 us
  matrix products: 11.3 us -> 0 us
    reduce_scatter x1 -> x0, waiting for transfers between devices: 99.4 us -> none  [local(): lax.psum_scatter(own_part.astype(jnp.float32).astype(jnp.bfloat16), 'dp',...]
    all_gather x1 -> x0, waiting for transfers between devices: 70.4 us -> none  [local(): weights = lax.all_gather(columns, 'dp', axis=0, tiled=True)]
    all_to_all x1, blocking collectives: 12 us -> 52.8 us  [local(): lax.all_to_all(spread.reshape(chips * tensors, own_rows, width), GROUP, s...]
    all_to_all x1, waiting for transfers between devices: 0.01 us -> 38.1 us  [local(): lax.all_to_all(pieces, GROUP, split_axis=0, concat_axis=0, tiled=True)]
    pallas_call x0 -> x4, Pallas kernels: none -> 12.9 us  [the longest x1 6.5 us: adam(): pl.pallas_call(adam_kernel, out_shape=(whole, whole, whole, jax.ShapeDtyp...]
    dot_general x1 -> x0, matrix products: 11.3 us -> none  [local(): jnp.einsum('s,srf->rf', slot_weight.astype(jnp.bfloat16), noise_draws, pr...]
    ppermute x0 -> x2, waiting for transfers between devices: none -> 10.6 us  [the longest x1 6.38 us: local(): received = lax.ppermute(given, 'core', SWAP)]
    all_to_all x1, starting transfers between devices: 4.13 us -> 11.6 us  [local(): lax.all_to_all(pieces, GROUP, split_axis=0, concat_axis=0, tiled=True)]
  transfers between devices with their start and end apart: 3 -> 3, of which waited for: 2 -> 3; matrix products, arithmetic and copies ran while one was open for 5% -> 0% of each run, Pallas kernels for 0% -> 3%
where the time goes in v1:
time: 148 us
  blocking collectives  52.8 us (36%)
  waiting for transfers between devices  48.7 us (33%)
  starting transfers between devices  17.4 us (12%)
  Pallas kernels  12.9 us (9%)
  local copies, waits for them, and re-layouts  8.39 us (6%)
  other arithmetic  5.99 us (4%)
    all_to_all x1, blocking collectives, local(): lax.all_to_all(spread.reshape(chips * tensors, own_rows, width), GROUP, s...  52.8 us
    all_to_all x1, waiting for transfers between devices, local(): lax.all_to_all(pieces, GROUP, split_axis=0, concat_axis=0, tiled=True)  38.1 us
    all_to_all x1, starting transfers between devices, local(): lax.all_to_all(pieces, GROUP, split_axis=0, concat_axis=0, tiled=True)  11.6 us
    pallas_call x1, Pallas kernels, adam(): pl.pallas_call(adam_kernel, out_shape=(whole, whole, whole, jax.ShapeDtyp...  6.5 us
    ppermute x1, waiting for transfers between devices, local(): received = lax.ppermute(given, 'core', SWAP)  6.38 us
    convert_element_type x1, other arithmetic, local(): (kept.astype(jnp.float32) + received.astype(jnp.float32)).astype(jnp.bflo...  5.97 us
    ppermute x1, starting transfers between devices, local(): other = lax.ppermute(gathered, 'core', SWAP)  4.43 us
    unnamed x12, local copies, waits for them, and re-layouts  4.27 us
  transfers between devices with their start and end apart: 3, of which 3 were waited for; matrix products, arithmetic and copies ran while one was open for 0% of the time, Pallas kernels for 3%

profile of v1, /device:TPU:1, one launch (start us, length us, event | category | flops | bytes accessed | tf_op | source)
XLA Modules:
  0.0 147.5 jit_solution(8066086706901797550)
XLA Ops:
  0.6 4.1 %dynamic-slice_bitcast_fusion = bf16[8,64,3584]{2,1,0:T(8,128)(2,1)} fusion(bf16[8,2,64,3584]{3,2,1,0:T(8,128)(2,1)} %bitcast.19, s32[]{:T(128)S(6)} %select_n.8), kind=kLoop, calls=%fused_computation.2 | loop fusion | bytes 7340036 | tf_op jit(solution)/shard_map/jit(dynamic_index_in_dim)/squeeze | solution.py:116
  4.8 1.4 collective-permute-start
  6.2 6.4 %collective-permute-done = bf16[8,64,3584]{2,1,0:T(8,128)(2,1)} collective-permute-done((bf16[8,64,3584]{2,1,0:T(8,128)(2,1)}, bf16[8,64,3584]{2,1,0:T(8,128)(2,1)}, u32[]{:S(2)}, u32[]{:S(2)}) %collective-permute-start) | collective-permute-done | bytes 3670048 | tf_op jit(solution)/shard_map/ppermute | solution.py:118
  12.6 6.0 %fusion = bf16[8,64,3584]{2,1,0:T(8,128)(2,1)} fusion(bf16[8,64,3584]{2,1,0:T(8,128)(2,1)} %collective-permute-done, bf16[8,2,64,3584]{3,2,1,0:T(8,128)(2,1)} %bitcast.20, s32[]{:T(128)S(6)} %select_n.7), kind=kLoop, calls=%fused_computation.1 | loop fusion | flops 7340032 | bytes 11010052 | tf_op jit(solution)/shard_map/convert_element_type | solution.py:119
  18.5 0.0 copy-start.4
  18.5 11.6 %all-to-all-start = ((bf16[64,8,3584]{2,1,0:T(8,128)(2,1)}), bf16[64,8,3584]{2,1,0:T(8,128)(2,1)}, u32[]{:S(2)}, u32[]{:S(2)}) async-start(bf16[64,8,3584]{2,1,0:T(8,128)(2,1)} %bitcast.18), calls=%async_computation | async-start | bytes 7340032 | tf_op jit(solution)/shard_map/all_to_all | solution.py:122
  30.8 0.0 copy-done.4
  30.8 0.0 copy-start
  30.8 3.1 %copy-done = bf16[16,8,28672]{2,1,0:T(8,128)(2,1)S(1)} copy-done((bf16[16,8,28672]{2,1,0:T(8,128)(2,1)S(1)}, bf16[16,8,28672]{2,1,0:T(8,128)(2,1)}, u32[]{:S(2)}) %copy-start) | copy-done | bytes 7340056
  33.9 0.0 copy-start.5
  33.9 0.0 copy-start.1
  33.9 0.0 copy-start.2
  33.9 2.7 %noise_sum.1.noise_ref = f32[8,28672]{1,0:T(8,128)S(1)} custom-call(s32[16]{0:T(128)S(1)} %copy-done.4, s32[1]{0:T(128)S(6)} %copy.14.step_ref, bf16[16,8,28672]{2,1,0:T(8,128)(2,1)S(1)} %copy-done), custom_call_target="tpu_custom_call" | custom-call | flops 7340032 | bytes 7340032 | tf_op jit(solution)/shard_map/noise_sum/pallas_call | solution.py:30
  36.5 0.0 copy-done.5
  36.6 38.1 %all-to-all-done = bf16[64,8,3584]{2,1,0:T(8,128)(2,1)} async-done(((bf16[64,8,3584]{2,1,0:T(8,128)(2,1)}), bf16[64,8,3584]{2,1,0:T(8,128)(2,1)}, u32[]{:S(2)}, u32[]{:S(2)}) %all-to-all-start) | async-done | bytes 3670048 | tf_op jit(solution)/shard_map/all_to_all | solution.py:122
  74.7 0.0 copy-done.1
  74.7 0.0 copy-done.2
  74.7 0.0 copy-start.3
  74.7 1.2 copy-done.3
  75.9 6.5 %adam.1 = (f32[8,28672]{1,0:T(8,128)}, f32[8,28672]{1,0:T(8,128)}, f32[8,28672]{1,0:T(8,128)}, bf16[8,8,8,3584]{3,2,1,0:T(8,128)(2,1)S(1)}) custom-call(f32[2]{0:T(128)S(1)} %power_subtract_fusion.correct_ref, bf16[8,8,8,3584]{3,2,1,0:T(8,128)(2,1)} %bitcast.5.sums_ref, f32[8,28672]{1,0:T(8,128)S(1)} %noise_sum.1.noise_ref, f32[8,28672]{1,0:T(8,128)S(1)} %copy-done.1, ...), custom_call_target="tpu_custom_call" | custom-call | tf_op jit(solution)/shard_map/adam/pallas_call | solution.py:75
  82.4 52.8 %all_to_all.10 = bf16[64,8,3584]{2,1,0:T(8,128)(2,1)S(1)} all-to-all(bf16[64,8,3584]{2,1,0:T(8,128)(2,1)S(1)} %bitcast.16), channel_id=1, replica_groups=mesh['z_hi'=2,'x'=4,'core'=2,'y'=4,'z_lo'=2] {'z_hi','x','y','z_lo'}, dimensions={0} | all-to-all | bytes 7340032 | tf_op jit(solution)/shard_map/all_to_all | solution.py:132
  135.2 4.4 %collective-permute-start.1 = (bf16[8,64,3584]{2,1,0:T(8,128)(2,1)S(1)}, bf16[8,64,3584]{2,1,0:T(8,128)(2,1)S(1)}, u32[]{:S(2)}, u32[]{:S(2)}) collective-permute-start(bf16[8,64,3584]{2,1,0:T(8,128)(2,1)S(1)} %bitcast.14), channel_id=1, source_target_pairs={{0,8},{8,0},{1,9},{9,1},{2,10},{10,2},{3,11},{11,3},{4,12},{12,4},... | collective-permute-start | bytes 11010056 | tf_op jit(solution)/shard_map/ppermute | solution.py:135
  139.6 1.8 %place.2.refs_0_ = bf16[8,2,64,3584]{3,2,1,0:T(8,128)(2,1)} custom-call(s32[1]{0:T(128)} %bitcast.9.side_ref, bf16[8,64,3584]{2,1,0:T(8,128)(2,1)S(1)} %bitcast.15), custom_call_target="tpu_custom_call" | custom-call | bytes 7340032 | tf_op jit(solution)/shard_map/place/pallas_call | solution.py:97
  141.5 4.2 %collective-permute-done.1.block_ref = bf16[8,64,3584]{2,1,0:T(8,128)(2,1)S(1)} collective-permute-done((bf16[8,64,3584]{2,1,0:T(8,128)(2,1)S(1)}, bf16[8,64,3584]{2,1,0:T(8,128)(2,1)S(1)}, u32[]{:S(2)}, u32[]{:S(2)}) %collective-permute-start.1) | collective-permute-done | bytes 3670048 | tf_op jit(solution)/shard_map/ppermute | solution.py:135
  145.7 1.8 %place.3 = bf16[8,2,64,3584]{3,2,1,0:T(8,128)(2,1)} custom-call(s32[1]{0:T(128)} %bitcast.6.side_ref, bf16[8,64,3584]{2,1,0:T(8,128)(2,1)S(1)} %collective-permute-done.1.block_ref, bf16[8,2,64,3584]{3,2,1,0:T(8,128)(2,1)} %place.2.refs_0_), custom_call_target="tpu_custom_call", output_to_operand_aliasing={{}: (2, {})} | custom-call | bytes 7340032 | tf_op jit(solution)/shard_map/place/pallas_call | solution.py:97
  (1 shorter events, 0.0 us)
Async XLA Ops:
  4.8 7.8 %collective-permute-start = (bf16[8,64,3584]{2,1,0:T(8,128)(2,1)}, bf16[8,64,3584]{2,1,0:T(8,128)(2,1)}, u32[]{:S(2)}, u32[]{:S(2)}) collective-permute-start(bf16[8,64,3584]{2,1,0:T(8,128)(2,1)} %dynamic-slice_bitcast_fusion), channel_id=1, source_target_pairs={{0,8},{8,0},{1,9},{9,1},{2,10},{10,2},{3,11},{11,3},{4,12},{12,4},... | collective-permute-start | bytes 11010056 | tf_op jit(solution)/shard_map/ppermute | solution.py:118
  18.5 12.2 %copy-start.4 = (s32[16]{0:T(128)S(1)}, s32[16]{0:T(128)}, u32[]{:S(2)}) copy-start(s32[16]{0:T(128)} %coeffs_ref.1) | copy-start | bytes 196
  18.5 56.1 %all-to-all-start = ((bf16[64,8,3584]{2,1,0:T(8,128)(2,1)}), bf16[64,8,3584]{2,1,0:T(8,128)(2,1)}, u32[]{:S(2)}, u32[]{:S(2)}) async-start(bf16[64,8,3584]{2,1,0:T(8,128)(2,1)} %bitcast.18), calls=%async_computation | async-start | bytes 7340032 | tf_op jit(solution)/shard_map/all_to_all | solution.py:122
  30.8 3.1 %copy-start = (bf16[16,8,28672]{2,1,0:T(8,128)(2,1)S(1)}, bf16[16,8,28672]{2,1,0:T(8,128)(2,1)}, u32[]{:S(2)}) copy-start(bf16[16,8,28672]{2,1,0:T(8,128)(2,1)} %draws_ref.1) | copy-start | bytes 22020100
  33.9 2.7 %copy-start.5 = (f32[2]{0:T(128)S(1)}, f32[2]{0:T(128)}, u32[]{:S(2)}) copy-start(f32[2]{0:T(128)} %constant.24.clone) | copy-start | bytes 28
  33.9 40.8 %copy-start.1 = (f32[8,28672]{1,0:T(8,128)S(1)}, f32[8,28672]{1,0:T(8,128)}, u32[]{:S(2)}) copy-start(f32[8,28672]{1,0:T(8,128)} %master_ref.1) | copy-start | bytes 2752516
  33.9 40.8 %copy-start.2 = (f32[8,28672]{1,0:T(8,128)S(1)}, f32[8,28672]{1,0:T(8,128)}, u32[]{:S(2)}) copy-start(f32[8,28672]{1,0:T(8,128)} %first_ref.1) | copy-start | bytes 2752516
  74.7 1.2 copy-start.3
  135.2 10.5 %collective-permute-start.1 = (bf16[8,64,3584]{2,1,0:T(8,128)(2,1)S(1)}, bf16[8,64,3584]{2,1,0:T(8,128)(2,1)S(1)}, u32[]{:S(2)}, u32[]{:S(2)}) collective-permute-start(bf16[8,64,3584]{2,1,0:T(8,128)(2,1)S(1)} %bitcast.14), channel_id=1, source_target_pairs={{0,8},{8,0},{1,9},{9,1},{2,10},{10,2},{3,11},{11,3},{4,12},{12,4},... | collective-permute-start | bytes 11010056 | tf_op jit(solution)/shard_map/ppermute | solution.py:135

commit v2 on v0

v2 whole, which is shorter than its diff:
```python
import functools

import jax
import jax.numpy as jnp
from jax import lax
from jax.experimental import pallas as pl
from jax.experimental.pallas import tpu as pltpu
from jax.sharding import Mesh, PartitionSpec as P

HISTORY = 16
GROUP = ("z_hi", "x", "y", "z_lo")
DP = ("z_hi", "x", "core")
TENSOR = ("y", "z_lo")
Z, X, Y, T = 2, 4, 4, 8
VMEM_BYTES = 16 * 1024 * 1024
SMALL = 1024 * 1024
SMEM = pl.BlockSpec(memory_space=pltpu.SMEM)
ANY = pl.BlockSpec(memory_space=pl.ANY)
F32, BF16 = jnp.float32, jnp.bfloat16


def struct(shape, dtype):
    return jax.ShapeDtypeStruct(shape, dtype)


def in_hbm(array):
    return pltpu.with_memory_space_constraint(array, pltpu.HBM)


def in_vmem(array):
    return pltpu.with_memory_space_constraint(array, pltpu.VMEM)


def run_copies(copies, sems):
    started = [pltpu.make_async_copy(source, target, sems.at[i]) for i, (source, target) in enumerate(copies)]
    for copy in started:
        copy.start()
    for copy in started:
        copy.wait()


def copying(body, n, out_shape, n_in, aliases=None, moved=0, name=None):
    many = isinstance(out_shape, (tuple, list))

    def kernel(ids_ref, *refs):
        run_copies(body(ids_ref, refs[:n_in], refs[n_in:-1]), refs[-1])

    return pl.pallas_call(
        kernel,
        out_shape=out_shape,
        in_specs=[SMEM] + [ANY] * n_in,
        out_specs=[ANY] * len(out_shape) if many else ANY,
        scratch_shapes=[pltpu.SemaphoreType.DMA((n,))],
        input_output_aliases=aliases or {},
        compiler_params=pltpu.CompilerParams(vmem_limit_bytes=SMALL),
        cost_estimate=pl.CostEstimate(flops=0, bytes_accessed=moved, transcendentals=0),
        name=name,
    )


def split(ids, halves, other):
    chips, _, rows, columns = halves.shape

    def body(ids_ref, ins, outs):
        core = 1 - ids_ref[2] if other else ids_ref[2]
        return [(ins[0].at[i, core], outs[0].at[i]) for i in range(chips)]

    out = pltpu.VMEM((chips, rows, columns), BF16)
    name = "split_other" if other else "split_own"
    return copying(body, chips, [out], 1, moved=4 * chips * rows * columns, name=name)(ids, in_hbm(halves))[0]


def move(ids, arrays, space, name):
    def body(ids_ref, ins, outs):
        return list(zip(ins, outs))

    out = [space(a.shape, a.dtype) for a in arrays]
    moved = sum(2 * a.size * a.dtype.itemsize for a in arrays)
    return copying(body, len(arrays), out, len(arrays), moved=moved, name=name)(ids, *arrays)


def place(ids, block, other, into, name):
    chips, rows, columns = block.shape
    more = [] if into is None else [into]

    def body(ids_ref, ins, outs):
        core = 1 - ids_ref[2] if other else ids_ref[2]
        return [(ins[0].at[i], outs[0].at[i, core]) for i in range(chips)]

    out = struct((chips, 2, rows, columns), BF16)
    call = copying(body, chips, out, 1 + len(more), {2: 0} if more else {}, 4 * block.size, name)
    return call(ids, in_vmem(block), *more)


def noise_kernel(coeffs_ref, step_ref, draws_ref, noise_ref, held, sems):
    parts, width = held.shape[0], held.shape[-1]
    copies = [
        pltpu.make_async_copy(draws_ref.at[:, :, pl.ds(i * width, width)], held.at[i], sems.at[i])
        for i in range(parts)
    ]
    for copy in copies:
        copy.start()
    weights = [
        coeffs_ref[(step_ref[0] - slot) & (HISTORY - 1)].astype(F32) / 32.0 for slot in range(HISTORY)
    ]
    for i in range(parts):
        copies[i].wait()
        total = None
        for slot in range(HISTORY):
            term = weights[slot] * held[i, slot].astype(F32)
            total = term if total is None else total + term
        noise_ref[:, pl.ds(i * width, width)] = total


def noise_sum(band_coeffs, step, noise_draws):
    slots, rows, columns = noise_draws.shape
    return pl.pallas_call(
        noise_kernel,
        out_shape=[pltpu.VMEM((rows, columns), F32)],
        in_specs=[SMEM, SMEM, ANY],
        out_specs=[pl.BlockSpec(memory_space=pltpu.VMEM)],
        scratch_shapes=[
            pltpu.VMEM((T, slots, rows, columns // T), noise_draws.dtype), pltpu.SemaphoreType.DMA((T,)),
        ],
        compiler_params=pltpu.CompilerParams(vmem_limit_bytes=VMEM_BYTES),
        cost_estimate=pl.CostEstimate(
            flops=2 * slots * rows * columns, bytes_accessed=2 * slots * rows * columns, transcendentals=0
        ),
        name="noise_sum",
    )(band_coeffs, step, in_hbm(noise_draws))[0]


def adam(grad_sum, noise, master, first, second, correct_ref):
    gradient = 0.25 * (grad_sum + noise)
    new_first = 0.9 * first + 0.1 * gradient
    new_second = 0.95 * second + 0.05 * gradient * gradient
    update = new_first / correct_ref[0] / (jnp.sqrt(new_second / correct_ref[1]) + 1e-08) + 0.1 * master
    return master - 0.02 * update, new_first, new_second


def total_of(sums_ref):
    total = sums_ref[0, 0].astype(F32)
    for source in range(1, sums_ref.shape[0]):
        total = total + sums_ref[source, 0].astype(F32)
    return total


def adam_kernel(
    correct_ref, sums_ref, noise_ref, master_ref, first_ref, second_ref,
    new_master_ref, new_first_ref, new_second_ref, spread_ref,
):
    new_master, new_first_ref[...], new_second_ref[...] = adam(
        total_of(sums_ref), noise_ref[...], master_ref[...], first_ref[...], second_ref[...], correct_ref
    )
    new_master_ref[...] = new_master
    rounded = new_master.astype(BF16)
    for copy in range(spread_ref.shape[0]):
        spread_ref[copy, 0] = rounded


def adam_step(correct, sums, noise, master, first, second):
    sources, parts, rows, width = sums.shape
    state = pl.BlockSpec((rows, width), lambda i: (0, i))
    spread = pl.BlockSpec((sources, 1, rows, width), lambda i: (0, i, 0, 0))
    return pl.pallas_call(
        adam_kernel,
        out_shape=[pltpu.VMEM(master.shape, F32)] * 3 + [pltpu.VMEM(sums.shape, BF16)],
        grid=(parts,),
        in_specs=[SMEM, spread, state, state, state, state],
        out_specs=[state] * 3 + [spread],
        compiler_params=pltpu.CompilerParams(vmem_limit_bytes=VMEM_BYTES),
        name="adam_step",
    )(correct, in_vmem(sums), in_vmem(noise), in_vmem(master), in_vmem(first), in_vmem(second))


def swap(value, axis):
    return lax.ppermute(value, axis, [(0, 1), (1, 0)])


def plus_kernel(a_ref, b_ref, out_ref):
    out_ref[...] = (a_ref[...].astype(F32) + b_ref[...].astype(F32)).astype(BF16)


def plus(a, b):
    chips, rows, columns = a.shape
    block = pl.BlockSpec((1, rows, columns), lambda i: (i, 0, 0))
    return pl.pallas_call(
        plus_kernel,
        out_shape=[pltpu.VMEM(a.shape, BF16)],
        grid=(chips,),
        in_specs=[block, block],
        out_specs=[block],
        compiler_params=pltpu.CompilerParams(vmem_limit_bytes=VMEM_BYTES),
        name="plus",
    )(in_vmem(a), in_vmem(b))[0]


def local(partial_grads, master, first, second, noise_draws, band_coeffs, step):
    ids = jnp.stack([lax.axis_index(name) for name in ("z_hi", "x", "core", "y", "z_lo")]).astype(jnp.int32)
    _, rows, columns = partial_grads.shape
    block = rows // (2 * X * Z)
    own = block // T
    halves = partial_grads.reshape(Z * X, 2, block, columns)

    got = swap(split(ids, halves, True), "core")
    kept = split(ids, halves, False)

    noise = noise_sum(band_coeffs, step, noise_draws)
    count = (step[0] + 1).astype(F32)
    correct = 1.0 - jnp.power(jnp.array([0.9, 0.95], F32), count)

    pieces = plus(kept, got).reshape(Z * X * T, own, columns)
    pieces, noise, correct = lax.optimization_barrier((pieces, noise, correct))
    sums = lax.all_to_all(pieces, GROUP, split_axis=0, concat_axis=0, tiled=True).reshape(Z * X, T, own, columns)
    *states, spread = adam_step(correct, sums, noise, master, first, second)

    gathered = lax.all_to_all(
        spread.reshape(Z * X * T, own, columns), GROUP, split_axis=0, concat_axis=0, tiled=True
    ).reshape(Z * X, block, columns)
    gathered, states = lax.optimization_barrier((gathered, states))
    other = swap(gathered, "core")
    weights = place(ids, gathered, False, None, "place_own")
    new_master, new_first, new_second = move(ids, [in_vmem(a) for a in states], pltpu.HBM, "store_states")
    weights = place(ids, other, True, weights, "place_other")
    return (new_master, new_first, new_second, weights.reshape(rows, columns))


def solution(mesh):
    fine = Mesh(mesh.devices.reshape(Z, X, 2, Y, 2), ("z_hi", "x", "core", "y", "z_lo"))
    owners = DP + TENSOR
    return jax.shard_map(
        local,
        mesh=fine,
        in_specs=(
            P(DP, None, TENSOR),
            P(owners, None),
            P(owners, None),
            P(owners, None),
            P(None, owners, None),
            P(),
            P(),
        ),
        out_specs=(P(owners, None), P(owners, None), P(owners, None), P(None, TENSOR)),
        check_vma=False,
    )
```

time: 224 us -> 138 us (0.62)
  waiting for transfers between devices: 170 us -> 1.49 us
  blocking collectives: 12 us -> 110 us
  Pallas kernels: 0 us -> 19.6 us
  between operations: 14.8 us -> 1.42 us
  matrix products: 11.3 us -> 0 us
  local copies, waits for them, and re-layouts: 6.61 us -> 0.12 us
  other arithmetic: 3.98 us -> 0.02 us
    reduce_scatter x1 -> x0, waiting for transfers between devices: 99.4 us -> none  [local(): lax.psum_scatter(own_part.astype(jnp.float32).astype(jnp.bfloat16), 'dp',...]
    all_to_all x1 -> x2, blocking collectives: 12 us -> 110 us  [the longest x1 56.6 us: local(): lax.all_to_all(pieces, GROUP, split_axis=0, concat_axis=0, tiled=True)]
    all_gather x1 -> x0, waiting for transfers between devices: 70.4 us -> none  [local(): weights = lax.all_gather(columns, 'dp', axis=0, tiled=True)]
    pallas_call x0 -> x8, Pallas kernels: none -> 19.6 us  [the longest x2 5.2 us: split(): copying(body, chips, [out], 1, moved=4 * chips * rows * columns, name=name)]
    dot_general x1 -> x0, matrix products: 11.3 us -> none  [local(): jnp.einsum('s,srf->rf', slot_weight.astype(jnp.bfloat16), noise_draws, pr...]
    unnamed x7 -> x10, local copies, waits for them, and re-layouts: 6.61 us -> 0.03 us
    ppermute x0 -> x2, starting transfers between devices: none -> 4.45 us  [swap(): return lax.ppermute(value, axis, [(0, 1), (1, 0)])]
    all_to_all x1 -> x0, starting transfers between devices: 4.13 us -> none  [local(): lax.all_to_all(summed.astype(jnp.bfloat16), 'tensor', split_axis=0, conca...]
  transfers between devices with their start and end apart: 3 -> 2, of which waited for: 2 -> 1; matrix products, arithmetic and copies ran while one was open for 5% -> 0% of each run, Pallas kernels for 0% -> 8%
where the time goes in v2:
time: 138 us; the launch traced here: 137 us
  blocking collectives  110 us (80%)
  Pallas kernels  19.6 us (14%)
  starting transfers between devices  4.45 us (3%)
  waiting for transfers between devices  1.49 us (1%)
  between operations  1.42 us (1%)
    all_to_all x1, blocking collectives, local(): lax.all_to_all(pieces, GROUP, split_axis=0, concat_axis=0, tiled=True)  56.6 us
    all_to_all x1, blocking collectives, local(): lax.all_to_all(spread.reshape(Z * X * T, own, columns), GROUP, split_axis...  53.2 us
    pallas_call x2, Pallas kernels, split(): copying(body, chips, [out], 1, moved=4 * chips * rows * columns, name=name)  5.2 us
    pallas_call x2, Pallas kernels, place(): return call(ids, in_vmem(block), *more)  4.87 us
    ppermute x2, starting transfers between devices, swap(): return lax.ppermute(value, axis, [(0, 1), (1, 0)])  4.45 us
    pallas_call x1, Pallas kernels, noise_sum(): pl.pallas_call(noise_kernel, out_shape=[pltpu.VMEM((rows, columns), F32)]...  3.89 us
  transfers between devices with their start and end apart: 2, of which 1 were waited for; matrix products, arithmetic and copies ran while one was open for 0% of the time, Pallas kernels for 8%

profile of v2, /device:TPU:1, one launch (start us, length us, event | category | flops | bytes accessed | tf_op | source)
XLA Modules:
  0.0 136.9 jit_solution(17803594355215251838)
XLA Ops:
  0.6 0.1 stack.23.ids_ref
  0.7 2.6 %split_other.1 = bf16[8,64,3584]{2,1,0:T(8,128)(2,1)S(1)} custom-call(s32[5]{0:T(128)S(1)} %stack.23.ids_ref, bf16[8,2,64,3584]{3,2,1,0:T(8,128)(2,1)} %bitcast.17), custom_call_target="tpu_custom_call" | custom-call | bytes 7340032 | tf_op jit(solution)/shard_map/split_other/pallas_call | solution.py:70
  3.3 0.0 copy-start.3
  3.3 1.5 %collective-permute-start = (bf16[8,64,3584]{2,1,0:T(8,128)(2,1)S(1)}, bf16[8,64,3584]{2,1,0:T(8,128)(2,1)S(1)}, u32[]{:S(2)}, u32[]{:S(2)}) collective-permute-start(bf16[8,64,3584]{2,1,0:T(8,128)(2,1)S(1)} %split_other.1), channel_id=1, source_target_pairs={{0,8},{8,0},{1,9},{9,1},{2,10},{10,2},{3,11},{11,3},{4,12},{12,4},... | collective-permute-start | bytes 11010056 | tf_op jit(solution)/shard_map/ppermute | solution.py:177
  4.8 2.6 %split_own.1.a_ref = bf16[8,64,3584]{2,1,0:T(8,128)(2,1)S(1)} custom-call(s32[5]{0:T(128)S(1)} %stack.23.ids_ref, bf16[8,2,64,3584]{3,2,1,0:T(8,128)(2,1)} %bitcast.18), custom_call_target="tpu_custom_call" | custom-call | bytes 7340032 | tf_op jit(solution)/shard_map/split_own/pallas_call | solution.py:70
  8.1 0.0 copy-done.3
  8.1 0.0 copy-start.4
  8.1 3.9 %noise_sum.1.noise_ref = f32[8,28672]{1,0:T(8,128)S(1)} custom-call(s32[16]{0:T(128)S(1)} %copy-done.3, s32[1]{0:T(128)S(6)} %copy.14.step_ref, bf16[16,8,28672]{2,1,0:T(8,128)(2,1)} %draws_ref.1), custom_call_target="tpu_custom_call" | custom-call | flops 7340032 | bytes 7340032 | tf_op jit(solution)/shard_map/noise_sum/pallas_call | solution.py:117
  12.0 0.0 copy-done.4
  12.1 0.0 collective-permute-done.b_ref
  12.1 1.0 plus.1
  13.0 0.0 copy-start
  13.0 0.0 copy-start.1
  13.1 0.0 copy-start.2
  13.1 56.6 %all_to_all.10 = bf16[64,8,3584]{2,1,0:T(8,128)(2,1)S(1)} all-to-all(bf16[64,8,3584]{2,1,0:T(8,128)(2,1)S(1)} %bitcast.15), channel_id=1, replica_groups=mesh['z_hi'=2,'x'=4,'core'=2,'y'=4,'z_lo'=2] {'z_hi','x','y','z_lo'}, dimensions={0} | all-to-all | bytes 7340032 | tf_op jit(solution)/shard_map/all_to_all | solution.py:214
  69.7 0.0 copy-done
  69.7 0.0 copy-done.1
  69.7 0.0 copy-done.2
  69.7 2.6 %adam_step.1 = (f32[8,28672]{1,0:T(8,128)S(1)}, f32[8,28672]{1,0:T(8,128)S(1)}, f32[8,28672]{1,0:T(8,128)S(1)}, bf16[8,8,8,3584]{3,2,1,0:T(8,128)(2,1)S(1)}) custom-call(f32[2]{0:T(128)S(1)} %power_subtract_fusion.correct_ref, bf16[8,8,8,3584]{3,2,1,0:T(8,128)(2,1)S(1)} %bitcast.14, f32[8,28672]{1,0:T(8,128)S(1)} %noise_sum.1.noise_ref, ...), custom_call_target="tpu_custom_call" | custom-call | tf_op jit(solution)/shard_map/adam_step/pallas_call | solution.py:165
  72.3 53.2 %all_to_all.11 = bf16[64,8,3584]{2,1,0:T(8,128)(2,1)S(1)} all-to-all(bf16[64,8,3584]{2,1,0:T(8,128)(2,1)S(1)} %bitcast.16), channel_id=1, replica_groups=mesh['z_hi'=2,'x'=4,'core'=2,'y'=4,'z_lo'=2] {'z_hi','x','y','z_lo'}, dimensions={0} | all-to-all | bytes 7340032 | tf_op jit(solution)/shard_map/all_to_all | solution.py:217
  125.5 2.9 %collective-permute-start.1 = (bf16[8,64,3584]{2,1,0:T(8,128)(2,1)S(1)}, bf16[8,64,3584]{2,1,0:T(8,128)(2,1)S(1)}, u32[]{:S(2)}, u32[]{:S(2)}) collective-permute-start(bf16[8,64,3584]{2,1,0:T(8,128)(2,1)S(1)} %bitcast.12), channel_id=1, source_target_pairs={{0,8},{8,0},{1,9},{9,1},{2,10},{10,2},{3,11},{11,3},{4,12},{12,4},... | collective-permute-start | bytes 11010056 | tf_op jit(solution)/shard_map/ppermute | solution.py:177
  128.5 2.4 %place_own.1.refs_1_ = bf16[8,2,64,3584]{3,2,1,0:T(8,128)(2,1)} custom-call(s32[5]{0:T(128)S(1)} %stack.23.ids_ref, bf16[8,64,3584]{2,1,0:T(8,128)(2,1)S(1)} %bitcast.13), custom_call_target="tpu_custom_call" | custom-call | bytes 7340032 | tf_op jit(solution)/shard_map/place_own/pallas_call | solution.py:92
  130.9 2.1 %store_states.1 = (f32[8,28672]{1,0:T(8,128)}, f32[8,28672]{1,0:T(8,128)}, f32[8,28672]{1,0:T(8,128)}) custom-call(s32[5]{0:T(128)S(1)} %stack.23.ids_ref, f32[8,28672]{1,0:T(8,128)S(1)} %get-tuple-element.25.refs_0_, f32[8,28672]{1,0:T(8,128)S(1)} %get-tuple-element.26.refs_1_, f32[8,28672]{1,0:T(8,128)S(1)} %get-tuple-element.27.refs_2_), custom_call_target="tpu_custom_call" | custom-call | bytes 5505024 | tf_op jit(solution)/shard_map/store_states/pallas_call | solution.py:79
  133.0 1.5 %collective-permute-done.1.refs_0_ = bf16[8,64,3584]{2,1,0:T(8,128)(2,1)S(1)} collective-permute-done((bf16[8,64,3584]{2,1,0:T(8,128)(2,1)S(1)}, bf16[8,64,3584]{2,1,0:T(8,128)(2,1)S(1)}, u32[]{:S(2)}, u32[]{:S(2)}) %collective-permute-start.1) | collective-permute-done | bytes 3670048 | tf_op jit(solution)/shard_map/ppermute | solution.py:177
  134.5 2.4 %place_other.1 = bf16[8,2,64,3584]{3,2,1,0:T(8,128)(2,1)} custom-call(s32[5]{0:T(128)S(1)} %stack.23.ids_ref, bf16[8,64,3584]{2,1,0:T(8,128)(2,1)S(1)} %collective-permute-done.1.refs_0_, bf16[8,2,64,3584]{3,2,1,0:T(8,128)(2,1)} %place_own.1.refs_1_), custom_call_target="tpu_custom_call", output_to_operand_aliasing={{}: (2, {})} | custom-call | bytes 7340032 | tf_op jit(solution)/shard_map/place_other/pallas_call | solution.py:92
  (1 shorter events, 0.0 us)
Async XLA Ops:
  3.3 4.8 %copy-start.3 = (s32[16]{0:T(128)S(1)}, s32[16]{0:T(128)}, u32[]{:S(2)}) copy-start(s32[16]{0:T(128)} %coeffs_ref.1) | copy-start | bytes 196
  3.3 8.7 %collective-permute-start = (bf16[8,64,3584]{2,1,0:T(8,128)(2,1)S(1)}, bf16[8,64,3584]{2,1,0:T(8,128)(2,1)S(1)}, u32[]{:S(2)}, u32[]{:S(2)}) collective-permute-start(bf16[8,64,3584]{2,1,0:T(8,128)(2,1)S(1)} %split_other.1), channel_id=1, source_target_pairs={{0,8},{8,0},{1,9},{9,1},{2,10},{10,2},{3,11},{11,3},{4,12},{12,4},... | collective-permute-start | bytes 11010056 | tf_op jit(solution)/shard_map/ppermute | solution.py:177
  8.1 3.9 %copy-start.4 = (f32[2]{0:T(128)S(1)}, f32[2]{0:T(128)}, u32[]{:S(2)}) copy-start(f32[2]{0:T(128)} %constant.26.clone) | copy-start | bytes 28
  13.0 56.7 %copy-start = (f32[8,28672]{1,0:T(8,128)S(1)}, f32[8,28672]{1,0:T(8,128)}, u32[]{:S(2)}) copy-start(f32[8,28672]{1,0:T(8,128)} %master_ref.1) | copy-start | bytes 2752516
  13.0 56.6 %copy-start.1 = (f32[8,28672]{1,0:T(8,128)S(1)}, f32[8,28672]{1,0:T(8,128)}, u32[]{:S(2)}) copy-start(f32[8,28672]{1,0:T(8,128)} %first_ref.1) | copy-start | bytes 2752516
  13.1 56.6 %copy-start.2 = (f32[8,28672]{1,0:T(8,128)S(1)}, f32[8,28672]{1,0:T(8,128)}, u32[]{:S(2)}) copy-start(f32[8,28672]{1,0:T(8,128)} %second_ref.1) | copy-start | bytes 2752516
  125.5 9.0 %collective-permute-start.1 = (bf16[8,64,3584]{2,1,0:T(8,128)(2,1)S(1)}, bf16[8,64,3584]{2,1,0:T(8,128)(2,1)S(1)}, u32[]{:S(2)}, u32[]{:S(2)}) collective-permute-start(bf16[8,64,3584]{2,1,0:T(8,128)(2,1)S(1)} %bitcast.12), channel_id=1, source_target_pairs={{0,8},{8,0},{1,9},{9,1},{2,10},{10,2},{3,11},{11,3},{4,12},{12,4},... | collective-permute-start | bytes 11010056 | tf_op jit(solution)/shard_map/ppermute | solution.py:177

commit v3 on v2

--- a/solution.py
+++ b/solution.py
@@ -8,7 +8,7 @@
 from jax.sharding import Mesh, PartitionSpec as P
 
 HISTORY = 16
-GROUP = ("z_hi", "x", "y", "z_lo")
+GROUP = ("y", "z_lo", "z_hi", "x")
 DP = ("z_hi", "x", "core")
 TENSOR = ("y", "z_lo")
 Z, X, Y, T = 2, 4, 4, 8
@@ -58,16 +58,19 @@
     )
 
 
-def split(ids, halves, other):
-    chips, _, rows, columns = halves.shape
+def split(ids, halves, parts, name):
+    rows, columns = halves.shape[2:]
 
     def body(ids_ref, ins, outs):
-        core = 1 - ids_ref[2] if other else ids_ref[2]
-        return [(ins[0].at[i, core], outs[0].at[i]) for i in range(chips)]
-
-    out = pltpu.VMEM((chips, rows, columns), BF16)
-    name = "split_other" if other else "split_own"
-    return copying(body, chips, [out], 1, moved=4 * chips * rows * columns, name=name)(ids, in_hbm(halves))[0]
+        core = ids_ref[2]
+        return [
+            (ins[0].at[pl.ds(first, n), 1 - core if other else core], outs[i])
+            for i, (first, n, other) in enumerate(parts)
+        ]
+
+    out = [pltpu.VMEM((n, rows, columns), BF16) for _, n, _ in parts]
+    moved = 4 * rows * columns * sum(n for _, n, _ in parts)
+    return copying(body, len(parts), out, 1, moved=moved, name=name)(ids, in_hbm(halves))
 
 
 def move(ids, arrays, space, name):
@@ -79,55 +82,43 @@
     return copying(body, len(arrays), out, len(arrays), moved=moved, name=name)(ids, *arrays)
 
 
-def place(ids, block, other, into, name):
-    chips, rows, columns = block.shape
+def place(ids, pieces, other, into, name):
+    owners, chips, rows, columns = pieces.shape
     more = [] if into is None else [into]
 
     def body(ids_ref, ins, outs):
         core = 1 - ids_ref[2] if other else ids_ref[2]
-        return [(ins[0].at[i], outs[0].at[i, core]) for i in range(chips)]
-
-    out = struct((chips, 2, rows, columns), BF16)
-    call = copying(body, chips, out, 1 + len(more), {2: 0} if more else {}, 4 * block.size, name)
-    return call(ids, in_vmem(block), *more)
-
-
-def noise_kernel(coeffs_ref, step_ref, draws_ref, noise_ref, held, sems):
-    parts, width = held.shape[0], held.shape[-1]
-    copies = [
-        pltpu.make_async_copy(draws_ref.at[:, :, pl.ds(i * width, width)], held.at[i], sems.at[i])
-        for i in range(parts)
-    ]
-    for copy in copies:
-        copy.start()
-    weights = [
-        coeffs_ref[(step_ref[0] - slot) & (HISTORY - 1)].astype(F32) / 32.0 for slot in range(HISTORY)
-    ]
-    for i in range(parts):
-        copies[i].wait()
-        total = None
-        for slot in range(HISTORY):
-            term = weights[slot] * held[i, slot].astype(F32)
-            total = term if total is None else total + term
-        noise_ref[:, pl.ds(i * width, width)] = total
+        return [(ins[0].at[:, i], outs[0].at[i, core]) for i in range(chips)]
+
+    out = struct((chips, 2, owners, rows, columns), BF16)
+    call = copying(body, chips, out, 1 + len(more), {2: 0} if more else {}, 4 * pieces.size, name)
+    return call(ids, in_vmem(pieces), *more)
+
+
+def noise_kernel(coeffs_ref, step_ref, draws_ref, noise_ref):
+    total = None
+    for slot in range(HISTORY):
+        weight = coeffs_ref[(step_ref[0] - slot) & (HISTORY - 1)].astype(F32) / 32.0
+        term = weight * draws_ref[slot].astype(F32)
+        total = term if total is None else total + term
+    noise_ref[...] = total
 
 
 def noise_sum(band_coeffs, step, noise_draws):
     slots, rows, columns = noise_draws.shape
+    width = columns // T
     return pl.pallas_call(
         noise_kernel,
         out_shape=[pltpu.VMEM((rows, columns), F32)],
-        in_specs=[SMEM, SMEM, ANY],
-        out_specs=[pl.BlockSpec(memory_space=pltpu.VMEM)],
-        scratch_shapes=[
-            pltpu.VMEM((T, slots, rows, columns // T), noise_draws.dtype), pltpu.SemaphoreType.DMA((T,)),
-        ],
+        grid=(T,),
+        in_specs=[SMEM, SMEM, pl.BlockSpec((slots, rows, width), lambda i: (0, 0, i))],
+        out_specs=[pl.BlockSpec((rows, width), lambda i: (0, i))],
         compiler_params=pltpu.CompilerParams(vmem_limit_bytes=VMEM_BYTES),
         cost_estimate=pl.CostEstimate(
             flops=2 * slots * rows * columns, bytes_accessed=2 * slots * rows * columns, transcendentals=0
         ),
         name="noise_sum",
-    )(band_coeffs, step, in_hbm(noise_draws))[0]
+    )(band_coeffs, step, in_vmem(noise_draws))[0]
 
 
 def adam(grad_sum, noise, master, first, second, correct_ref):
@@ -140,8 +131,8 @@
 
 def total_of(sums_ref):
     total = sums_ref[0, 0].astype(F32)
-    for source in range(1, sums_ref.shape[0]):
-        total = total + sums_ref[source, 0].astype(F32)
+    for source in range(1, sums_ref.shape[1]):
+        total = total + sums_ref[0, source].astype(F32)
     return total
 
 
@@ -154,14 +145,14 @@
     )
     new_master_ref[...] = new_master
     rounded = new_master.astype(BF16)
-    for copy in range(spread_ref.shape[0]):
-        spread_ref[copy, 0] = rounded
+    for copy in range(spread_ref.shape[1]):
+        spread_ref[0, copy] = rounded
 
 
 def adam_step(correct, sums, noise, master, first, second):
-    sources, parts, rows, width = sums.shape
+    parts, sources, rows, width = sums.shape
     state = pl.BlockSpec((rows, width), lambda i: (0, i))
-    spread = pl.BlockSpec((sources, 1, rows, width), lambda i: (0, i, 0, 0))
+    spread = pl.BlockSpec((1, sources, rows, width), lambda i: (i, 0, 0, 0))
     return pl.pallas_call(
         adam_kernel,
         out_shape=[pltpu.VMEM(master.shape, F32)] * 3 + [pltpu.VMEM(sums.shape, BF16)],
@@ -177,22 +168,28 @@
     return lax.ppermute(value, axis, [(0, 1), (1, 0)])
 
 
-def plus_kernel(a_ref, b_ref, out_ref):
-    out_ref[...] = (a_ref[...].astype(F32) + b_ref[...].astype(F32)).astype(BF16)
-
-
-def plus(a, b):
-    chips, rows, columns = a.shape
+def plus_kernel(a_ref, b_ref, *refs):
+    out_ref = refs[-1]
+    owners, _, rows, _ = out_ref.shape
+    for t in range(owners):
+        cut = slice(t * rows, (t + 1) * rows)
+        out_ref[t, 0] = (a_ref[0, cut].astype(F32) + b_ref[0, cut].astype(F32)).astype(BF16)
+
+
+def plus(a, b, first, chips, into):
+    n, rows, columns = a.shape
     block = pl.BlockSpec((1, rows, columns), lambda i: (i, 0, 0))
+    more = [] if into is None else [into]
     return pl.pallas_call(
         plus_kernel,
-        out_shape=[pltpu.VMEM(a.shape, BF16)],
-        grid=(chips,),
-        in_specs=[block, block],
-        out_specs=[block],
+        out_shape=[pltpu.VMEM((T, chips, rows // T, columns), BF16)],
+        grid=(n,),
+        in_specs=[block, block] + [ANY] * len(more),
+        out_specs=[pl.BlockSpec((T, 1, rows // T, columns), lambda i: (0, first + i, 0, 0))],
+        input_output_aliases={2: 0} if more else {},
         compiler_params=pltpu.CompilerParams(vmem_limit_bytes=VMEM_BYTES),
         name="plus",
-    )(in_vmem(a), in_vmem(b))[0]
+    )(in_vmem(a), in_vmem(b), *more)[0]
 
 
 def local(partial_grads, master, first, second, noise_draws, band_coeffs, step):
@@ -202,21 +199,30 @@
     own = block // T
     halves = partial_grads.reshape(Z * X, 2, block, columns)
 
-    got = swap(split(ids, halves, True), "core")
-    kept = split(ids, halves, False)
+    chips = Z * X
+    half = chips // 2
+    (given_a,) = split(ids, halves, [(0, half, True)], "split_first")
+    got_a = swap(given_a, "core")
+    given_b, kept_a, kept_b = split(
+        ids, halves, [(half, half, True), (0, half, False), (half, half, False)], "split_rest"
+    )
+    got_b = swap(given_b, "core")
 
     noise = noise_sum(band_coeffs, step, noise_draws)
     count = (step[0] + 1).astype(F32)
     correct = 1.0 - jnp.power(jnp.array([0.9, 0.95], F32), count)
 
-    pieces = plus(kept, got).reshape(Z * X * T, own, columns)
+    pieces = plus(kept_a, got_a, 0, chips, None)
+    pieces = plus(kept_b, got_b, half, chips, pieces)
     pieces, noise, correct = lax.optimization_barrier((pieces, noise, correct))
-    sums = lax.all_to_all(pieces, GROUP, split_axis=0, concat_axis=0, tiled=True).reshape(Z * X, T, own, columns)
+    sums = lax.all_to_all(
+        pieces.reshape(T * chips, own, columns), GROUP, split_axis=0, concat_axis=0, tiled=True
+    ).reshape(T, chips, own, columns)
     *states, spread = adam_step(correct, sums, noise, master, first, second)
 
     gathered = lax.all_to_all(
-        spread.reshape(Z * X * T, own, columns), GROUP, split_axis=0, concat_axis=0, tiled=True
-    ).reshape(Z * X, block, columns)
+        spread.reshape(T * chips, own, columns), GROUP, split_axis=0, concat_axis=0, tiled=True
+    ).reshape(T, chips, own, columns)
     gathered, states = lax.optimization_barrier((gathered, states))
     other = swap(gathered, "core")
     weights = place(ids, gathered, False, None, "place_own")

time: 138 us -> 133 us (0.964)
  blocking collectives: 110 us -> 107 us
    all_to_all x2, blocking collectives: 110 us -> 107 us  [the longest x1 56.6 us: local(): lax.all_to_all(pieces.reshape(T * chips, own, columns), GROUP, split_axis...]
    pallas_call x5 -> x6, Pallas kernels: 11 us -> 11.6 us  [the longest x2 5.5 us: split(): copying(body, len(parts), out, 1, moved=moved, name=name)]
    ppermute x2 -> x3, starting transfers between devices: 4.45 us -> 4.05 us  [swap(): return lax.ppermute(value, axis, [(0, 1), (1, 0)])]
  transfers between devices with their start and end apart: 2 -> 3, of which waited for: 1 -> 1; matrix products, arithmetic and copies ran while one was open for 0% -> 0% of each run, Pallas kernels for 8% -> 8%
where the time goes in v3:
time: 133 us
  blocking collectives  107 us (80%)
  Pallas kernels  18.4 us (14%)
  starting transfers between devices  4.05 us (3%)
  waiting for transfers between devices  1.5 us (1%)
  between operations  1.46 us (1%)
    all_to_all x1, blocking collectives, local(): lax.all_to_all(pieces.reshape(T * chips, own, columns), GROUP, split_axis...  56.6 us
    all_to_all x1, blocking collectives, local(): lax.all_to_all(spread.reshape(T * chips, own, columns), GROUP, split_axis...  50.7 us
    pallas_call x2, Pallas kernels, split(): copying(body, len(parts), out, 1, moved=moved, name=name)  5.5 us
    pallas_call x2, Pallas kernels, place(): return call(ids, in_vmem(pieces), *more)  4.87 us
    ppermute x3, starting transfers between devices, swap(): return lax.ppermute(value, axis, [(0, 1), (1, 0)])  4.05 us
    pallas_call x1, Pallas kernels, noise_sum(): pl.pallas_call(noise_kernel, out_shape=[pltpu.VMEM((rows, columns), F32)]...  2.69 us
  transfers between devices with their start and end apart: 3, of which 1 were waited for; matrix products, arithmetic and copies ran while one was open for 0% of the time, Pallas kernels for 8%

profile of v3, /device:TPU:1, one launch (start us, length us, event | category | flops | bytes accessed | tf_op | source)
XLA Modules:
  0.0 132.8 jit_solution(8345500974522857135)
XLA Ops:
  0.6 0.1 stack.23.ids_ref
  0.7 0.0 slice-start
  0.7 0.0 slice-start.1
  0.7 2.3 %split_first.1 = bf16[4,64,3584]{2,1,0:T(8,128)(2,1)S(1)} custom-call(s32[5]{0:T(128)S(1)} %stack.23.ids_ref, bf16[8,2,64,3584]{3,2,1,0:T(8,128)(2,1)} %bitcast.19), custom_call_target="tpu_custom_call" | custom-call | bytes 3670016 | tf_op jit(solution)/shard_map/split_first/pallas_call | solution.py:73
  3.1 0.0 copy-start.3
  3.1 1.5 %collective-permute-start.1 = (bf16[4,64,3584]{2,1,0:T(8,128)(2,1)S(1)}, bf16[4,64,3584]{2,1,0:T(8,128)(2,1)S(1)}, u32[]{:S(2)}, u32[]{:S(2)}) collective-permute-start(bf16[4,64,3584]{2,1,0:T(8,128)(2,1)S(1)} %split_first.1), channel_id=1, source_target_pairs={{0,8},{8,0},{1,9},{9,1},{2,10},{10,2},{3,11},{11,3},{4,12},{12,4},... | collective-permute-start | bytes 5505032 | tf_op jit(solution)/shard_map/ppermute | solution.py:168
  4.6 3.2 %split_rest.1 = (bf16[4,64,3584]{2,1,0:T(8,128)(2,1)S(1)}, bf16[4,64,3584]{2,1,0:T(8,128)(2,1)S(1)}, bf16[4,64,3584]{2,1,0:T(8,128)(2,1)S(1)}) custom-call(s32[5]{0:T(128)S(1)} %stack.23.ids_ref, bf16[8,2,64,3584]{3,2,1,0:T(8,128)(2,1)} %bitcast.20), custom_call_target="tpu_custom_call" | custom-call | bytes 11010048 | tf_op jit(solution)/shard_map/split_rest/pallas_call | solution.py:73
  7.8 0.1 collective-permute-start
  8.5 0.0 slice-done
  8.5 0.0 slice-done.1
  8.5 0.0 copy-done.3
  8.5 0.0 copy-start.4
  8.6 2.7 %noise_sum.1.noise_ref = f32[8,28672]{1,0:T(8,128)S(1)} custom-call(s32[16]{0:T(128)S(1)} %copy-done.3, s32[1]{0:T(128)S(6)} %copy.16.step_ref, bf16[16,8,28672]{2,1,0:T(8,128)(2,1)S(1)} %bitcast.17), custom_call_target="tpu_custom_call" | custom-call | flops 7340032 | bytes 7340032 | tf_op jit(solution)/shard_map/noise_sum/pallas_call | solution.py:110
  11.2 0.0 copy-done.4
  11.3 0.0 collective-permute-done.1.b_ref
  11.3 0.6 plus.2.refs_0_
  11.9 0.0 collective-permute-done.b_ref
  11.9 0.6 plus.3
  12.5 0.0 copy-start
  12.6 0.0 copy-start.1
  12.6 0.0 copy-start.2
  12.6 56.6 %all_to_all.10 = bf16[64,8,3584]{2,1,0:T(8,128)(2,1)S(1)} all-to-all(bf16[64,8,3584]{2,1,0:T(8,128)(2,1)S(1)} %bitcast.12), channel_id=1, replica_groups=mesh['z_hi'=2,'x'=4,'core'=2,'y'=4,'z_lo'=2] {'y','z_lo','z_hi','x'}, dimensions={0} | all-to-all | bytes 7340032 | tf_op jit(solution)/shard_map/all_to_all | solution.py:218
  69.1 0.0 copy-done
  69.1 0.0 copy-done.1
  69.1 0.0 copy-done.2
  69.1 2.1 %adam_step.1 = (f32[8,28672]{1,0:T(8,128)S(1)}, f32[8,28672]{1,0:T(8,128)S(1)}, f32[8,28672]{1,0:T(8,128)S(1)}, bf16[8,8,8,3584]{3,2,1,0:T(8,128)(2,1)S(1)}) custom-call(f32[2]{0:T(128)S(1)} %power_subtract_fusion.correct_ref, bf16[8,8,8,3584]{3,2,1,0:T(8,128)(2,1)S(1)} %bitcast.15, f32[8,28672]{1,0:T(8,128)S(1)} %noise_sum.1.noise_ref, ...), custom_call_target="tpu_custom_call" | custom-call | tf_op jit(solution)/shard_map/adam_step/pallas_call | solution.py:156
  71.2 50.7 %all_to_all.11 = bf16[64,8,3584]{2,1,0:T(8,128)(2,1)S(1)} all-to-all(bf16[64,8,3584]{2,1,0:T(8,128)(2,1)S(1)} %bitcast.18), channel_id=1, replica_groups=mesh['z_hi'=2,'x'=4,'core'=2,'y'=4,'z_lo'=2] {'y','z_lo','z_hi','x'}, dimensions={0} | all-to-all | bytes 7340032 | tf_op jit(solution)/shard_map/all_to_all | solution.py:223
  121.9 2.5 %collective-permute-start.2 = (bf16[8,8,8,3584]{3,2,1,0:T(8,128)(2,1)S(1)}, bf16[8,8,8,3584]{3,2,1,0:T(8,128)(2,1)S(1)}, u32[]{:S(2)}, u32[]{:S(2)}) collective-permute-start(bf16[8,8,8,3584]{3,2,1,0:T(8,128)(2,1)S(1)} %bitcast.13), channel_id=1, source_target_pairs={{0,8},{8,0},{1,9},{9,1},{2,10},{10,2},{3,11},{11,3},{4,12},{12,4},... | collective-permute-start | bytes 11010056 | tf_op jit(solution)/shard_map/ppermute | solution.py:168
  124.3 2.4 %place_own.1.refs_1_ = bf16[8,2,8,8,3584]{4,3,2,1,0:T(8,128)(2,1)} custom-call(s32[5]{0:T(128)S(1)} %stack.23.ids_ref, bf16[8,8,8,3584]{3,2,1,0:T(8,128)(2,1)S(1)} %bitcast.14), custom_call_target="tpu_custom_call" | custom-call | bytes 7340032 | tf_op jit(solution)/shard_map/place_own/pallas_call | solution.py:95
  126.8 2.1 %store_states.1 = (f32[8,28672]{1,0:T(8,128)}, f32[8,28672]{1,0:T(8,128)}, f32[8,28672]{1,0:T(8,128)}) custom-call(s32[5]{0:T(128)S(1)} %stack.23.ids_ref, f32[8,28672]{1,0:T(8,128)S(1)} %get-tuple-element.31.refs_0_, f32[8,28672]{1,0:T(8,128)S(1)} %get-tuple-element.32.refs_1_, f32[8,28672]{1,0:T(8,128)S(1)} %get-tuple-element.33.refs_2_), custom_call_target="tpu_custom_call" | custom-call | bytes 5505024 | tf_op jit(solution)/shard_map/store_states/pallas_call | solution.py:82
  128.9 1.5 %collective-permute-done.2.refs_0_ = bf16[8,8,8,3584]{3,2,1,0:T(8,128)(2,1)S(1)} collective-permute-done((bf16[8,8,8,3584]{3,2,1,0:T(8,128)(2,1)S(1)}, bf16[8,8,8,3584]{3,2,1,0:T(8,128)(2,1)S(1)}, u32[]{:S(2)}, u32[]{:S(2)}) %collective-permute-start.2) | collective-permute-done | bytes 3670048 | tf_op jit(solution)/shard_map/ppermute | solution.py:168
  130.4 2.4 %place_other.1 = bf16[8,2,8,8,3584]{4,3,2,1,0:T(8,128)(2,1)} custom-call(s32[5]{0:T(128)S(1)} %stack.23.ids_ref, bf16[8,8,8,3584]{3,2,1,0:T(8,128)(2,1)S(1)} %collective-permute-done.2.refs_0_, bf16[8,2,8,8,3584]{4,3,2,1,0:T(8,128)(2,1)} %place_own.1.refs_1_), custom_call_target="tpu_custom_call", output_to_operand_aliasing={{}: (2, {})} | custom-call | bytes 7340032 | tf_op jit(solution)/shard_map/place_other/pallas_call | solution.py:95
  (2 shorter events, 0.0 us)
Async XLA Ops:
  0.7 7.8 %slice-start = ((s8[7340032]{0:T(1024)(128)(4,1)}), s8[4194304]{0:T(1024)(128)(4,1)S(1)}, s32[]{:S(2)}) async-start(s8[7340032]{0:T(1024)(128)(4,1)} %bitcast.16), calls=%async_computation.2 | async-start | bytes 8388608
  0.7 7.8 %slice-start.1 = ((s8[7340032]{0:T(1024)(128)(4,1)}), s8[3145728]{0:T(1024)(128)(4,1)S(1)}, s32[]{:S(2)}) async-start(s8[7340032]{0:T(1024)(128)(4,1)} %bitcast.16), calls=%async_computation.3 | async-start | bytes 6291456
  3.1 5.5 %copy-start.3 = (s32[16]{0:T(128)S(1)}, s32[16]{0:T(128)}, u32[]{:S(2)}) copy-start(s32[16]{0:T(128)} %coeffs_ref.1) | copy-start | bytes 196
  3.1 8.2 %collective-permute-start.1 = (bf16[4,64,3584]{2,1,0:T(8,128)(2,1)S(1)}, bf16[4,64,3584]{2,1,0:T(8,128)(2,1)S(1)}, u32[]{:S(2)}, u32[]{:S(2)}) collective-permute-start(bf16[4,64,3584]{2,1,0:T(8,128)(2,1)S(1)} %split_first.1), channel_id=1, source_target_pairs={{0,8},{8,0},{1,9},{9,1},{2,10},{10,2},{3,11},{11,3},{4,12},{12,4},... | collective-permute-start | bytes 5505032 | tf_op jit(solution)/shard_map/ppermute | solution.py:168
  7.8 4.2 %collective-permute-start = (bf16[4,64,3584]{2,1,0:T(8,128)(2,1)S(1)}, bf16[4,64,3584]{2,1,0:T(8,128)(2,1)S(1)}, u32[]{:S(2)}, u32[]{:S(2)}) collective-permute-start(bf16[4,64,3584]{2,1,0:T(8,128)(2,1)S(1)} %get-tuple-element.22), channel_id=1, source_target_pairs={{0,8},{8,0},{1,9},{9,1},{2,10},{10,2},{3,11},{11,3},{4,12},{12,4},... | collective-permute-start | bytes 5505032 | tf_op jit(solution)/shard_map/ppermute | solution.py:168
  8.5 2.7 %copy-start.4 = (f32[2]{0:T(128)S(1)}, f32[2]{0:T(128)}, u32[]{:S(2)}) copy-start(f32[2]{0:T(128)} %constant.26.clone) | copy-start | bytes 28
  12.5 56.6 %copy-start = (f32[8,28672]{1,0:T(8,128)S(1)}, f32[8,28672]{1,0:T(8,128)}, u32[]{:S(2)}) copy-start(f32[8,28672]{1,0:T(8,128)} %master_ref.1) | copy-start | bytes 2752516
  12.6 56.6 %copy-start.1 = (f32[8,28672]{1,0:T(8,128)S(1)}, f32[8,28672]{1,0:T(8,128)}, u32[]{:S(2)}) copy-start(f32[8,28672]{1,0:T(8,128)} %first_ref.1) | copy-start | bytes 2752516
  12.6 56.6 %copy-start.2 = (f32[8,28672]{1,0:T(8,128)S(1)}, f32[8,28672]{1,0:T(8,128)}, u32[]{:S(2)}) copy-start(f32[8,28672]{1,0:T(8,128)} %second_ref.1) | copy-start | bytes 2752516
  121.9 8.5 %collective-permute-start.2 = (bf16[8,8,8,3584]{3,2,1,0:T(8,128)(2,1)S(1)}, bf16[8,8,8,3584]{3,2,1,0:T(8,128)(2,1)S(1)}, u32[]{:S(2)}, u32[]{:S(2)}) collective-permute-start(bf16[8,8,8,3584]{3,2,1,0:T(8,128)(2,1)S(1)} %bitcast.13), channel_id=1, source_target_pairs={{0,8},{8,0},{1,9},{9,1},{2,10},{10,2},{3,11},{11,3},{4,12},{12,4},... | collective-permute-start | bytes 11010056 | tf_op jit(solution)/shard_map/ppermute | solution.py:168

commit v4 on v3

--- a/solution.py
+++ b/solution.py
@@ -12,10 +12,12 @@
 DP = ("z_hi", "x", "core")
 TENSOR = ("y", "z_lo")
 Z, X, Y, T = 2, 4, 4, 8
+EARLY = 5
 VMEM_BYTES = 16 * 1024 * 1024
 SMALL = 1024 * 1024
 SMEM = pl.BlockSpec(memory_space=pltpu.SMEM)
 ANY = pl.BlockSpec(memory_space=pl.ANY)
+VMEM = pl.BlockSpec(memory_space=pltpu.VMEM)
 F32, BF16 = jnp.float32, jnp.bfloat16
 
 
@@ -73,46 +75,54 @@
     return copying(body, len(parts), out, 1, moved=moved, name=name)(ids, in_hbm(halves))
 
 
-def move(ids, arrays, space, name):
+def place_own(ids, pieces, states):
+    owners, chips, rows, columns = pieces.shape
+
     def body(ids_ref, ins, outs):
-        return list(zip(ins, outs))
-
-    out = [space(a.shape, a.dtype) for a in arrays]
-    moved = sum(2 * a.size * a.dtype.itemsize for a in arrays)
-    return copying(body, len(arrays), out, len(arrays), moved=moved, name=name)(ids, *arrays)
-
-
-def place(ids, pieces, other, into, name):
-    owners, chips, rows, columns = pieces.shape
-    more = [] if into is None else [into]
+        copies = [(ins[0].at[:, i], outs[0].at[i, ids_ref[2]]) for i in range(chips)]
+        return copies + list(zip(ins[1:], outs[1:]))
+
+    out = [pltpu.HBM((chips, 2, owners, rows, columns), BF16)] + [pltpu.HBM(a.shape, a.dtype) for a in states]
+    moved = 4 * pieces.size + sum(8 * a.size for a in states)
+    call = copying(body, chips + len(states), out, 1 + len(states), moved=moved, name="place_own")
+    return call(ids, *[in_vmem(a) for a in (pieces, *states)])
+
+
+def place_other(ids, pieces, first, into, name):
+    n = pieces.shape[0]
 
     def body(ids_ref, ins, outs):
-        core = 1 - ids_ref[2] if other else ids_ref[2]
-        return [(ins[0].at[:, i], outs[0].at[i, core]) for i in range(chips)]
-
-    out = struct((chips, 2, owners, rows, columns), BF16)
-    call = copying(body, chips, out, 1 + len(more), {2: 0} if more else {}, 4 * pieces.size, name)
-    return call(ids, in_vmem(pieces), *more)
+        return [(ins[0].at[t], outs[0].at[:, 1 - ids_ref[2], first + t]) for t in range(n)]
+
+    call = copying(body, n, struct(into.shape, BF16), 2, {2: 0}, 4 * pieces.size, name)
+    return call(ids, in_vmem(pieces), into)
 
 
 def noise_kernel(coeffs_ref, step_ref, draws_ref, noise_ref):
-    total = None
-    for slot in range(HISTORY):
-        weight = coeffs_ref[(step_ref[0] - slot) & (HISTORY - 1)].astype(F32) / 32.0
-        term = weight * draws_ref[slot].astype(F32)
-        total = term if total is None else total + term
-    noise_ref[...] = total
+    weights = [
+        coeffs_ref[(step_ref[0] - slot) & (HISTORY - 1)].astype(F32) / 32.0 for slot in range(HISTORY)
+    ]
+    width = 3584
+
+    def part(i, carry):
+        cut = pl.ds(pl.multiple_of(i * width, width), width)
+        total = None
+        for slot in range(HISTORY):
+            term = weights[slot] * draws_ref[slot, :, cut].astype(F32)
+            total = term if total is None else total + term
+        noise_ref[:, cut] = total
+        return carry
+
+    lax.fori_loop(0, noise_ref.shape[1] // width, part, 0)
 
 
 def noise_sum(band_coeffs, step, noise_draws):
     slots, rows, columns = noise_draws.shape
-    width = columns // T
     return pl.pallas_call(
         noise_kernel,
         out_shape=[pltpu.VMEM((rows, columns), F32)],
-        grid=(T,),
-        in_specs=[SMEM, SMEM, pl.BlockSpec((slots, rows, width), lambda i: (0, 0, i))],
-        out_specs=[pl.BlockSpec((rows, width), lambda i: (0, i))],
+        in_specs=[SMEM, SMEM, VMEM],
+        out_specs=[VMEM],
         compiler_params=pltpu.CompilerParams(vmem_limit_bytes=VMEM_BYTES),
         cost_estimate=pl.CostEstimate(
             flops=2 * slots * rows * columns, bytes_accessed=2 * slots * rows * columns, transcendentals=0
@@ -224,10 +234,11 @@
         spread.reshape(T * chips, own, columns), GROUP, split_axis=0, concat_axis=0, tiled=True
     ).reshape(T, chips, own, columns)
     gathered, states = lax.optimization_barrier((gathered, states))
-    other = swap(gathered, "core")
-    weights = place(ids, gathered, False, None, "place_own")
-    new_master, new_first, new_second = move(ids, [in_vmem(a) for a in states], pltpu.HBM, "store_states")
-    weights = place(ids, other, True, weights, "place_other")
+    other_a = swap(gathered[:EARLY], "core")
+    other_b = swap(gathered[EARLY:], "core")
+    weights, new_master, new_first, new_second = place_own(ids, gathered, states)
+    weights = place_other(ids, other_a, 0, weights, "place_early")
+    weights = place_other(ids, other_b, EARLY, weights, "place_late")
     return (new_master, new_first, new_second, weights.reshape(rows, columns))
 
 

time: 133 us -> 132 us (level)
    ppermute x3 -> x4, starting transfers between devices: 4.05 us -> 4.52 us  [swap(): return lax.ppermute(value, axis, [(0, 1), (1, 0)])]
  transfers between devices with their start and end apart: 3 -> 4, of which waited for: 1 -> 2; matrix products, arithmetic and copies ran while one was open for 0% -> 0% of each run, Pallas kernels for 8% -> 8%
where the time goes in v4:
time: 132 us
  blocking collectives  107 us (81%)
  Pallas kernels  17.8 us (13%)
  starting transfers between devices  4.52 us (3%)
  between operations  1.48 us (1%)
    all_to_all x1, blocking collectives, local(): lax.all_to_all(pieces.reshape(T * chips, own, columns), GROUP, split_axis...  56.9 us
    all_to_all x1, blocking collectives, local(): lax.all_to_all(spread.reshape(T * chips, own, columns), GROUP, split_axis...  50.3 us
    pallas_call x2, Pallas kernels, split(): copying(body, len(parts), out, 1, moved=moved, name=name)  5.5 us
    ppermute x4, starting transfers between devices, swap(): return lax.ppermute(value, axis, [(0, 1), (1, 0)])  4.52 us
    pallas_call x2, Pallas kernels, place_other(): return call(ids, in_vmem(pieces), into)  3.6 us
    pallas_call x1, Pallas kernels, place_own(): return call(ids, *[in_vmem(a) for a in (pieces, *states)])  3.35 us
  transfers between devices with their start and end apart: 4, of which 2 were waited for; matrix products, arithmetic and copies ran while one was open for 0% of the time, Pallas kernels for 8%

profile of v4, /device:TPU:1, one launch (start us, length us, event | category | flops | bytes accessed | tf_op | source)
XLA Modules:
  0.0 132.3 jit_solution(6500180232928828483)
XLA Ops:
  0.6 0.1 stack.23.ids_ref
  0.7 0.0 slice-start
  0.7 0.0 slice-start.1
  0.7 2.3 %split_first.1 = bf16[4,64,3584]{2,1,0:T(8,128)(2,1)S(1)} custom-call(s32[5]{0:T(128)S(1)} %stack.23.ids_ref, bf16[8,2,64,3584]{3,2,1,0:T(8,128)(2,1)} %bitcast.21), custom_call_target="tpu_custom_call" | custom-call | bytes 3670016 | tf_op jit(solution)/shard_map/split_first/pallas_call | solution.py:75
  3.1 0.0 copy-start.3
  3.1 1.5 %collective-permute-start.1 = (bf16[4,64,3584]{2,1,0:T(8,128)(2,1)S(1)}, bf16[4,64,3584]{2,1,0:T(8,128)(2,1)S(1)}, u32[]{:S(2)}, u32[]{:S(2)}) collective-permute-start(bf16[4,64,3584]{2,1,0:T(8,128)(2,1)S(1)} %split_first.1), channel_id=1, source_target_pairs={{0,8},{8,0},{1,9},{9,1},{2,10},{10,2},{3,11},{11,3},{4,12},{12,4},... | collective-permute-start | bytes 5505032 | tf_op jit(solution)/shard_map/ppermute | solution.py:178
  4.6 3.2 %split_rest.1 = (bf16[4,64,3584]{2,1,0:T(8,128)(2,1)S(1)}, bf16[4,64,3584]{2,1,0:T(8,128)(2,1)S(1)}, bf16[4,64,3584]{2,1,0:T(8,128)(2,1)S(1)}) custom-call(s32[5]{0:T(128)S(1)} %stack.23.ids_ref, bf16[8,2,64,3584]{3,2,1,0:T(8,128)(2,1)} %bitcast.22), custom_call_target="tpu_custom_call" | custom-call | bytes 11010048 | tf_op jit(solution)/shard_map/split_rest/pallas_call | solution.py:75
  7.8 0.1 collective-permute-start
  8.5 0.0 slice-done
  8.5 0.0 slice-done.1
  8.5 0.0 copy-done.3
  8.5 0.0 copy-start.4
  8.6 2.0 %noise_sum.1.noise_ref = f32[8,28672]{1,0:T(8,128)S(1)} custom-call(s32[16]{0:T(128)S(1)} %copy-done.3, s32[1]{0:T(128)S(6)} %copy.18.step_ref, bf16[16,8,28672]{2,1,0:T(8,128)(2,1)S(1)} %bitcast.18), custom_call_target="tpu_custom_call" | custom-call | flops 7340032 | bytes 7340032 | tf_op jit(solution)/shard_map/noise_sum/pallas_call | solution.py:121
  10.6 0.0 copy-done.4
  10.6 0.0 collective-permute-done.1.b_ref
  10.6 0.6 plus.2.refs_0_
  11.3 0.4 collective-permute-done.b_ref
  11.6 0.6 plus.3
  12.2 0.0 copy-start
  12.2 0.0 copy-start.1
  12.2 0.0 copy-start.2
  12.2 56.9 %all_to_all.10 = bf16[64,8,3584]{2,1,0:T(8,128)(2,1)S(1)} all-to-all(bf16[64,8,3584]{2,1,0:T(8,128)(2,1)S(1)} %bitcast.15), channel_id=1, replica_groups=mesh['z_hi'=2,'x'=4,'core'=2,'y'=4,'z_lo'=2] {'y','z_lo','z_hi','x'}, dimensions={0} | all-to-all | bytes 7340032 | tf_op jit(solution)/shard_map/all_to_all | solution.py:228
  69.2 0.0 copy-done
  69.2 0.0 copy-done.1
  69.2 0.0 copy-done.2
  69.2 2.1 %adam_step.1 = (f32[8,28672]{1,0:T(8,128)S(1)}, f32[8,28672]{1,0:T(8,128)S(1)}, f32[8,28672]{1,0:T(8,128)S(1)}, bf16[8,8,8,3584]{3,2,1,0:T(8,128)(2,1)S(1)}) custom-call(f32[2]{0:T(128)S(1)} %power_subtract_fusion.correct_ref, bf16[8,8,8,3584]{3,2,1,0:T(8,128)(2,1)S(1)} %bitcast.16, f32[8,28672]{1,0:T(8,128)S(1)} %noise_sum.1.noise_ref, ...), custom_call_target="tpu_custom_call" | custom-call | tf_op jit(solution)/shard_map/adam_step/pallas_call | solution.py:166
  71.3 50.3 %all_to_all.11 = bf16[64,8,3584]{2,1,0:T(8,128)(2,1)S(1)} all-to-all(bf16[64,8,3584]{2,1,0:T(8,128)(2,1)S(1)} %bitcast.19), channel_id=1, replica_groups=mesh['z_hi'=2,'x'=4,'core'=2,'y'=4,'z_lo'=2] {'y','z_lo','z_hi','x'}, dimensions={0} | all-to-all | bytes 7340032 | tf_op jit(solution)/shard_map/all_to_all | solution.py:233
  121.5 0.2 slice.7
  121.7 2.8 %collective-permute-start.3 = (bf16[5,8,8,3584]{3,2,1,0:T(8,128)(2,1)S(1)}, bf16[5,8,8,3584]{3,2,1,0:T(8,128)(2,1)S(1)}, u32[]{:S(2)}, u32[]{:S(2)}) collective-permute-start(bf16[5,8,8,3584]{3,2,1,0:T(8,128)(2,1)S(1)} %slice.7), channel_id=1, source_target_pairs={{0,8},{8,0},{1,9},{9,1},{2,10},{10,2},{3,11},{11,3},{4,12},{12,4},... | collective-permute-start | bytes 6881288 | tf_op jit(solution)/shard_map/ppermute | solution.py:178
  124.6 0.1 slice.6
  124.7 0.1 collective-permute-start.2
  124.8 3.3 %place_own.1 = (bf16[8,2,8,8,3584]{4,3,2,1,0:T(8,128)(2,1)}, f32[8,28672]{1,0:T(8,128)}, f32[8,28672]{1,0:T(8,128)}, f32[8,28672]{1,0:T(8,128)}) custom-call(s32[5]{0:T(128)S(1)} %stack.23.ids_ref, bf16[8,8,8,3584]{3,2,1,0:T(8,128)(2,1)S(1)} %bitcast.14, f32[8,28672]{1,0:T(8,128)S(1)} %get-tuple-element.33.refs_1_, ...), custom_call_target="tpu_custom_call" | custom-call | bytes 12845056 | tf_op jit(solution)/shard_map/place_own/pallas_call | solution.py:88
  128.1 0.5 collective-permute-done.3.refs_0_
  128.6 2.0 %place_early.1.refs_1_ = bf16[8,2,8,8,3584]{4,3,2,1,0:T(8,128)(2,1)} custom-call(s32[5]{0:T(128)S(1)} %stack.23.ids_ref, bf16[5,8,8,3584]{3,2,1,0:T(8,128)(2,1)S(1)} %collective-permute-done.3.refs_0_, bf16[8,2,8,8,3584]{4,3,2,1,0:T(8,128)(2,1)} %get-tuple-element.39.refs_1_), custom_call_target="tpu_custom_call", output_to_operand_aliasing={{}: (2, {})} | custom-call | bytes 4587520 | tf_op jit(solution)/shard_map/place_early/pallas_call | solution.py:98
  130.6 0.0 collective-permute-done.2.refs_0_
  130.6 1.6 %place_late.1 = bf16[8,2,8,8,3584]{4,3,2,1,0:T(8,128)(2,1)} custom-call(s32[5]{0:T(128)S(1)} %stack.23.ids_ref, bf16[3,8,8,3584]{3,2,1,0:T(8,128)(2,1)S(1)} %collective-permute-done.2.refs_0_, bf16[8,2,8,8,3584]{4,3,2,1,0:T(8,128)(2,1)} %place_early.1.refs_1_), custom_call_target="tpu_custom_call", output_to_operand_aliasing={{}: (2, {})} | custom-call | bytes 2752512 | tf_op jit(solution)/shard_map/place_late/pallas_call | solution.py:98
  (2 shorter events, 0.0 us)
Async XLA Ops:
  0.7 7.8 %slice-start = ((s8[7340032]{0:T(1024)(128)(4,1)}), s8[4194304]{0:T(1024)(128)(4,1)S(1)}, s32[]{:S(2)}) async-start(s8[7340032]{0:T(1024)(128)(4,1)} %bitcast.17), calls=%async_computation.2 | async-start | bytes 8388608
  0.7 7.8 %slice-start.1 = ((s8[7340032]{0:T(1024)(128)(4,1)}), s8[3145728]{0:T(1024)(128)(4,1)S(1)}, s32[]{:S(2)}) async-start(s8[7340032]{0:T(1024)(128)(4,1)} %bitcast.17), calls=%async_computation.3 | async-start | bytes 6291456
  3.1 5.5 %copy-start.3 = (s32[16]{0:T(128)S(1)}, s32[16]{0:T(128)}, u32[]{:S(2)}) copy-start(s32[16]{0:T(128)} %coeffs_ref.1) | copy-start | bytes 196
  3.1 7.6 %collective-permute-start.1 = (bf16[4,64,3584]{2,1,0:T(8,128)(2,1)S(1)}, bf16[4,64,3584]{2,1,0:T(8,128)(2,1)S(1)}, u32[]{:S(2)}, u32[]{:S(2)}) collective-permute-start(bf16[4,64,3584]{2,1,0:T(8,128)(2,1)S(1)} %split_first.1), channel_id=1, source_target_pairs={{0,8},{8,0},{1,9},{9,1},{2,10},{10,2},{3,11},{11,3},{4,12},{12,4},... | collective-permute-start | bytes 5505032 | tf_op jit(solution)/shard_map/ppermute | solution.py:178
  7.8 3.9 %collective-permute-start = (bf16[4,64,3584]{2,1,0:T(8,128)(2,1)S(1)}, bf16[4,64,3584]{2,1,0:T(8,128)(2,1)S(1)}, u32[]{:S(2)}, u32[]{:S(2)}) collective-permute-start(bf16[4,64,3584]{2,1,0:T(8,128)(2,1)S(1)} %get-tuple-element.23), channel_id=1, source_target_pairs={{0,8},{8,0},{1,9},{9,1},{2,10},{10,2},{3,11},{11,3},{4,12},{12,4},... | collective-permute-start | bytes 5505032 | tf_op jit(solution)/shard_map/ppermute | solution.py:178
  8.5 2.1 %copy-start.4 = (f32[2]{0:T(128)S(1)}, f32[2]{0:T(128)}, u32[]{:S(2)}) copy-start(f32[2]{0:T(128)} %constant.26.clone) | copy-start | bytes 28
  12.2 57.0 %copy-start = (f32[8,28672]{1,0:T(8,128)S(1)}, f32[8,28672]{1,0:T(8,128)}, u32[]{:S(2)}) copy-start(f32[8,28672]{1,0:T(8,128)} %master_ref.1) | copy-start | bytes 2752516
  12.2 56.9 %copy-start.1 = (f32[8,28672]{1,0:T(8,128)S(1)}, f32[8,28672]{1,0:T(8,128)}, u32[]{:S(2)}) copy-start(f32[8,28672]{1,0:T(8,128)} %first_ref.1) | copy-start | bytes 2752516
  12.2 56.9 %copy-start.2 = (f32[8,28672]{1,0:T(8,128)S(1)}, f32[8,28672]{1,0:T(8,128)}, u32[]{:S(2)}) copy-start(f32[8,28672]{1,0:T(8,128)} %second_ref.1) | copy-start | bytes 2752516
  121.7 6.9 %collective-permute-start.3 = (bf16[5,8,8,3584]{3,2,1,0:T(8,128)(2,1)S(1)}, bf16[5,8,8,3584]{3,2,1,0:T(8,128)(2,1)S(1)}, u32[]{:S(2)}, u32[]{:S(2)}) collective-permute-start(bf16[5,8,8,3584]{3,2,1,0:T(8,128)(2,1)S(1)} %slice.7), channel_id=1, source_target_pairs={{0,8},{8,0},{1,9},{9,1},{2,10},{10,2},{3,11},{11,3},{4,12},{12,4},... | collective-permute-start | bytes 6881288 | tf_op jit(solution)/shard_map/ppermute | solution.py:178
  124.7 5.9 %collective-permute-start.2 = (bf16[3,8,8,3584]{3,2,1,0:T(8,128)(2,1)S(1)}, bf16[3,8,8,3584]{3,2,1,0:T(8,128)(2,1)S(1)}, u32[]{:S(2)}, u32[]{:S(2)}) collective-permute-start(bf16[3,8,8,3584]{3,2,1,0:T(8,128)(2,1)S(1)} %slice.6), channel_id=1, source_target_pairs={{0,8},{8,0},{1,9},{9,1},{2,10},{10,2},{3,11},{11,3},{4,12},{12,4},... | collective-permute-start | bytes 4128776 | tf_op jit(solution)/shard_map/ppermute | solution.py:178

commit v5 on v4

--- a/solution.py
+++ b/solution.py
@@ -178,28 +178,56 @@
     return lax.ppermute(value, axis, [(0, 1), (1, 0)])
 
 
-def plus_kernel(a_ref, b_ref, *refs):
-    out_ref = refs[-1]
+def plus_kernel(n_ids, *refs):
+    a_ref, b_ref, out_ref = refs[n_ids], refs[n_ids + 1], refs[-1]
     owners, _, rows, _ = out_ref.shape
     for t in range(owners):
         cut = slice(t * rows, (t + 1) * rows)
         out_ref[t, 0] = (a_ref[0, cut].astype(F32) + b_ref[0, cut].astype(F32)).astype(BF16)
 
 
-def plus(a, b, first, chips, into):
+def plus(a, b, first, chips, into=None, ids=None):
     n, rows, columns = a.shape
     block = pl.BlockSpec((1, rows, columns), lambda i: (i, 0, 0))
     more = [] if into is None else [into]
-    return pl.pallas_call(
-        plus_kernel,
+    wait = [] if ids is None else [ids]
+    return pl.pallas_call(
+        functools.partial(plus_kernel, len(wait)),
         out_shape=[pltpu.VMEM((T, chips, rows // T, columns), BF16)],
         grid=(n,),
-        in_specs=[block, block] + [ANY] * len(more),
+        in_specs=[SMEM] * len(wait) + [block, block] + [ANY] * len(more),
         out_specs=[pl.BlockSpec((T, 1, rows // T, columns), lambda i: (0, first + i, 0, 0))],
-        input_output_aliases={2: 0} if more else {},
+        input_output_aliases={len(wait) + 2: 0} if more else {},
         compiler_params=pltpu.CompilerParams(vmem_limit_bytes=VMEM_BYTES),
         name="plus",
-    )(in_vmem(a), in_vmem(b), *more)[0]
+    )(*wait, in_vmem(a), in_vmem(b), *more)[0]
+
+
+TURN = (("z_hi", "x", "y"), ("x", "y"))
+MESH = ("z_hi", "x", "core", "y", "z_lo")
+SIZES = {"z_hi": Z, "x": X, "core": 2, "y": Y, "z_lo": 2}
+
+
+def index_of(place):
+    index = 0
+    for name in MESH:
+        index = index * SIZES[name] + place[name]
+    return index
+
+
+def after_turn(ids, ready):
+    token = ids.astype(F32) + 0.0 * ready.reshape(-1)[: ids.shape[0]].astype(F32)
+    for axes in TURN:
+        pairs = []
+        for flat in range(2 * X * Z * T):
+            place, rest = {}, flat
+            for name in reversed(MESH):
+                place[name], rest = rest % SIZES[name], rest // SIZES[name]
+            if place["core"] == 1:
+                across = dict(place, **{a: (place[a] + SIZES[a] // 2) % SIZES[a] for a in axes})
+                pairs.append((flat, index_of(across)))
+        token = lax.ppermute(token, MESH, pairs)
+    return ids + (token < 0.0).astype(jnp.int32)
 
 
 def local(partial_grads, master, first, second, noise_draws, band_coeffs, step):
@@ -222,8 +250,8 @@
     count = (step[0] + 1).astype(F32)
     correct = 1.0 - jnp.power(jnp.array([0.9, 0.95], F32), count)
 
-    pieces = plus(kept_a, got_a, 0, chips, None)
-    pieces = plus(kept_b, got_b, half, chips, pieces)
+    pieces = plus(kept_a, got_a, 0, chips)
+    pieces = plus(kept_b, got_b, half, chips, pieces, after_turn(ids, got_a[0, 0, :8]))
     pieces, noise, correct = lax.optimization_barrier((pieces, noise, correct))
     sums = lax.all_to_all(
         pieces.reshape(T * chips, own, columns), GROUP, split_axis=0, concat_axis=0, tiled=True

time: 132 us -> 124 us (0.939)
  blocking collectives: 107 us -> 81.9 us
  starting transfers between devices: 4.52 us -> 19.3 us
  waiting for transfers between devices: 0.87 us -> 2.53 us
    ppermute x0 -> x2, starting transfers between devices: none -> 17 us  [after_turn(): token = lax.ppermute(token, MESH, pairs)]
    all_to_all x1, blocking collectives: 56.9 us -> 41.6 us  [local(): lax.all_to_all(pieces.reshape(T * chips, own, columns), GROUP, split_axis...]
    all_to_all x1, blocking collectives: 50.3 us -> 40.3 us  [local(): lax.all_to_all(spread.reshape(T * chips, own, columns), GROUP, split_axis...]
    ppermute x4, starting transfers between devices: 4.52 us -> 2.26 us  [swap(): return lax.ppermute(value, axis, [(0, 1), (1, 0)])]
    ppermute x0 -> x2, waiting for transfers between devices: none -> 2.14 us  [after_turn(): token = lax.ppermute(token, MESH, pairs)]
  transfers between devices with their start and end apart: 4 -> 6, of which waited for: 2 -> 3; matrix products, arithmetic and copies ran while one was open for 0% -> 0% of each run, Pallas kernels for 8% -> 9%
where the time goes in v5:
time: 124 us
  blocking collectives  81.9 us (66%)
  starting transfers between devices  19.3 us (16%)
  Pallas kernels  18.3 us (15%)
  waiting for transfers between devices  2.53 us (2%)
  between operations  1.51 us (1%)
    all_to_all x1, blocking collectives, local(): lax.all_to_all(pieces.reshape(T * chips, own, columns), GROUP, split_axis...  41.6 us
    all_to_all x1, blocking collectives, local(): lax.all_to_all(spread.reshape(T * chips, own, columns), GROUP, split_axis...  40.3 us
    ppermute x2, starting transfers between devices, after_turn(): token = lax.ppermute(token, MESH, pairs)  17 us
    pallas_call x2, Pallas kernels, split(): copying(body, len(parts), out, 1, moved=moved, name=name)  5.5 us
    pallas_call x2, Pallas kernels, place_other(): return call(ids, in_vmem(pieces), into)  3.6 us
    pallas_call x1, Pallas kernels, place_own(): return call(ids, *[in_vmem(a) for a in (pieces, *states)])  3.34 us
  transfers between devices with their start and end apart: 6, of which 3 were waited for; matrix products, arithmetic and copies ran while one was open for 0% of the time, Pallas kernels for 9%

profile of v5, /device:TPU:1, one launch (start us, length us, event | category | flops | bytes accessed | tf_op | source)
XLA Modules:
  0.0 124.0 jit_solution(13906600879884637369)
XLA Ops:
  0.6 0.1 stack.23.ids_ref
  0.7 0.0 slice-start
  0.7 0.0 slice-start.1
  0.7 2.3 %split_first.1 = bf16[4,64,3584]{2,1,0:T(8,128)(2,1)S(1)} custom-call(s32[5]{0:T(128)S(1)} %stack.23.ids_ref, bf16[8,2,64,3584]{3,2,1,0:T(8,128)(2,1)} %bitcast.25), custom_call_target="tpu_custom_call" | custom-call | bytes 3670016 | tf_op jit(solution)/shard_map/split_first/pallas_call | solution.py:75
  3.1 0.0 copy-start.3
  3.1 1.5 %collective-permute-start = (bf16[4,64,3584]{2,1,0:T(8,128)(2,1)S(1)}, bf16[4,64,3584]{2,1,0:T(8,128)(2,1)S(1)}, u32[]{:S(2)}, u32[]{:S(2)}) collective-permute-start(bf16[4,64,3584]{2,1,0:T(8,128)(2,1)S(1)} %split_first.1), channel_id=1, source_target_pairs={{0,8},{8,0},{1,9},{9,1},{2,10},{10,2},{3,11},{11,3},{4,12},{12,4},... | collective-permute-start | bytes 5505032 | tf_op jit(solution)/shard_map/ppermute | solution.py:178
  4.6 3.2 %split_rest.1 = (bf16[4,64,3584]{2,1,0:T(8,128)(2,1)S(1)}, bf16[4,64,3584]{2,1,0:T(8,128)(2,1)S(1)}, bf16[4,64,3584]{2,1,0:T(8,128)(2,1)S(1)}) custom-call(s32[5]{0:T(128)S(1)} %stack.23.ids_ref, bf16[8,2,64,3584]{3,2,1,0:T(8,128)(2,1)} %bitcast.26), custom_call_target="tpu_custom_call" | custom-call | bytes 11010048 | tf_op jit(solution)/shard_map/split_rest/pallas_call | solution.py:75
  7.8 0.1 collective-permute-start.3
  8.5 0.0 slice-done
  8.5 0.0 slice-done.1
  8.5 0.0 copy-done.3
  8.5 0.0 copy-start.4
  8.6 2.0 %noise_sum.1.noise_ref = f32[8,28672]{1,0:T(8,128)S(1)} custom-call(s32[16]{0:T(128)S(1)} %copy-done.3, s32[1]{0:T(128)S(6)} %copy.18.step_ref, bf16[16,8,28672]{2,1,0:T(8,128)(2,1)S(1)} %bitcast.22), custom_call_target="tpu_custom_call" | custom-call | flops 7340032 | bytes 7340032 | tf_op jit(solution)/shard_map/noise_sum/pallas_call | solution.py:121
  10.6 0.0 copy-done.4
  10.6 0.0 collective-permute-done.refs_1_
  10.7 10.7 %collective-permute-start.1 = (f32[5]{0:T(128)S(1)}, f32[5]{0:T(128)S(1)}, u32[]{:S(2)}, u32[]{:S(2)}) collective-permute-start(f32[5]{0:T(128)S(1)} %fusion.3), channel_id=1, source_target_pairs={{8,108},{9,109},{10,110},{11,111},{12,104},{13,105},{14,106},{15,1... | collective-permute-start | bytes 68 | tf_op jit(solution)/shard_map/ppermute | solution.py:229
  21.3 0.6 plus.2.refs_3_
  22.0 0.3 collective-permute-done.1
  22.3 6.3 %collective-permute-start.2 = (f32[5]{0:T(128)S(1)}, f32[5]{0:T(128)S(1)}, u32[]{:S(2)}, u32[]{:S(2)}) collective-permute-start(f32[5]{0:T(128)S(1)} %collective-permute-done.1), channel_id=1, source_target_pairs={{8,44},{9,45},{10,46},{11,47},{12,40},{13,41},{14,42},{15,43},{24,... | collective-permute-start | bytes 68 | tf_op jit(solution)/shard_map/ppermute | solution.py:229
  28.6 1.8 %collective-permute-done.2 = f32[5]{0:T(128)S(1)} collective-permute-done((f32[5]{0:T(128)S(1)}, f32[5]{0:T(128)S(1)}, u32[]{:S(2)}, u32[]{:S(2)}) %collective-permute-start.2) | collective-permute-done | bytes 52 | tf_op jit(solution)/shard_map/ppermute | solution.py:229
  30.5 0.0 collective-permute-done.3.refs_2_
  30.5 1.2 plus.3
  31.7 0.0 copy-start
  31.7 0.0 copy-start.1
  31.7 0.0 copy-start.2
  31.7 41.6 %all_to_all.10 = bf16[64,8,3584]{2,1,0:T(8,128)(2,1)S(1)} all-to-all(bf16[64,8,3584]{2,1,0:T(8,128)(2,1)S(1)} %bitcast.16), channel_id=1, replica_groups=mesh['z_hi'=2,'x'=4,'core'=2,'y'=4,'z_lo'=2] {'y','z_lo','z_hi','x'}, dimensions={0} | all-to-all | bytes 7340032 | tf_op jit(solution)/shard_map/all_to_all | solution.py:256
  73.3 0.0 copy-done
  73.3 0.0 copy-done.1
  73.3 0.0 copy-done.2
  73.3 2.1 %adam_step.1 = (f32[8,28672]{1,0:T(8,128)S(1)}, f32[8,28672]{1,0:T(8,128)S(1)}, f32[8,28672]{1,0:T(8,128)S(1)}, bf16[8,8,8,3584]{3,2,1,0:T(8,128)(2,1)S(1)}) custom-call(f32[2]{0:T(128)S(1)} %power_subtract_fusion.correct_ref, bf16[8,8,8,3584]{3,2,1,0:T(8,128)(2,1)S(1)} %bitcast.20, f32[8,28672]{1,0:T(8,128)S(1)} %noise_sum.1.noise_ref, ...), custom_call_target="tpu_custom_call" | custom-call | tf_op jit(solution)/shard_map/adam_step/pallas_call | solution.py:166
  75.4 40.3 %all_to_all.11 = bf16[64,8,3584]{2,1,0:T(8,128)(2,1)S(1)} all-to-all(bf16[64,8,3584]{2,1,0:T(8,128)(2,1)S(1)} %bitcast.23), channel_id=1, replica_groups=mesh['z_hi'=2,'x'=4,'core'=2,'y'=4,'z_lo'=2] {'y','z_lo','z_hi','x'}, dimensions={0} | all-to-all | bytes 7340032 | tf_op jit(solution)/shard_map/all_to_all | solution.py:261
  115.6 0.2 slice.14
  115.8 0.1 collective-permute-start.5
  115.9 0.1 slice.13
  116.1 0.6 collective-permute-start.4
  116.6 3.3 %place_own.1 = (bf16[8,2,8,8,3584]{4,3,2,1,0:T(8,128)(2,1)}, f32[8,28672]{1,0:T(8,128)}, f32[8,28672]{1,0:T(8,128)}, f32[8,28672]{1,0:T(8,128)}) custom-call(s32[5]{0:T(128)S(1)} %stack.23.ids_ref, bf16[8,8,8,3584]{3,2,1,0:T(8,128)(2,1)S(1)} %bitcast.19, f32[8,28672]{1,0:T(8,128)S(1)} %get-tuple-element.33.refs_1_, ...), custom_call_target="tpu_custom_call" | custom-call | bytes 12845056 | tf_op jit(solution)/shard_map/place_own/pallas_call | solution.py:88
  120.0 0.4 collective-permute-done.5.refs_0_
  120.4 2.0 %place_early.1.refs_1_ = bf16[8,2,8,8,3584]{4,3,2,1,0:T(8,128)(2,1)} custom-call(s32[5]{0:T(128)S(1)} %stack.23.ids_ref, bf16[5,8,8,3584]{3,2,1,0:T(8,128)(2,1)S(1)} %collective-permute-done.5.refs_0_, bf16[8,2,8,8,3584]{4,3,2,1,0:T(8,128)(2,1)} %get-tuple-element.39.refs_1_), custom_call_target="tpu_custom_call", output_to_operand_aliasing={{}: (2, {})} | custom-call | bytes 4587520 | tf_op jit(solution)/shard_map/place_early/pallas_call | solution.py:98
  122.3 0.0 collective-permute-done.4.refs_0_
  122.3 1.6 %place_late.1 = bf16[8,2,8,8,3584]{4,3,2,1,0:T(8,128)(2,1)} custom-call(s32[5]{0:T(128)S(1)} %stack.23.ids_ref, bf16[3,8,8,3584]{3,2,1,0:T(8,128)(2,1)S(1)} %collective-permute-done.4.refs_0_, bf16[8,2,8,8,3584]{4,3,2,1,0:T(8,128)(2,1)} %place_early.1.refs_1_), custom_call_target="tpu_custom_call", output_to_operand_aliasing={{}: (2, {})} | custom-call | bytes 2752512 | tf_op jit(solution)/shard_map/place_late/pallas_call | solution.py:98
  (4 shorter events, 0.0 us)
Async XLA Ops:
  0.7 7.8 %slice-start = ((s8[7340032]{0:T(1024)(128)(4,1)}), s8[4194304]{0:T(1024)(128)(4,1)S(1)}, s32[]{:S(2)}) async-start(s8[7340032]{0:T(1024)(128)(4,1)} %bitcast.21), calls=%async_computation.2 | async-start | bytes 8388608
  0.7 7.8 %slice-start.1 = ((s8[7340032]{0:T(1024)(128)(4,1)}), s8[3145728]{0:T(1024)(128)(4,1)S(1)}, s32[]{:S(2)}) async-start(s8[7340032]{0:T(1024)(128)(4,1)} %bitcast.21), calls=%async_computation.3 | async-start | bytes 6291456
  3.1 5.5 %copy-start.3 = (s32[16]{0:T(128)S(1)}, s32[16]{0:T(128)}, u32[]{:S(2)}) copy-start(s32[16]{0:T(128)} %coeffs_ref.1) | copy-start | bytes 196
  3.1 7.6 %collective-permute-start = (bf16[4,64,3584]{2,1,0:T(8,128)(2,1)S(1)}, bf16[4,64,3584]{2,1,0:T(8,128)(2,1)S(1)}, u32[]{:S(2)}, u32[]{:S(2)}) collective-permute-start(bf16[4,64,3584]{2,1,0:T(8,128)(2,1)S(1)} %split_first.1), channel_id=1, source_target_pairs={{0,8},{8,0},{1,9},{9,1},{2,10},{10,2},{3,11},{11,3},{4,12},{12,4},... | collective-permute-start | bytes 5505032 | tf_op jit(solution)/shard_map/ppermute | solution.py:178
  7.8 22.7 %collective-permute-start.3 = (bf16[4,64,3584]{2,1,0:T(8,128)(2,1)S(1)}, bf16[4,64,3584]{2,1,0:T(8,128)(2,1)S(1)}, u32[]{:S(2)}, u32[]{:S(2)}) collective-permute-start(bf16[4,64,3584]{2,1,0:T(8,128)(2,1)S(1)} %get-tuple-element.23), channel_id=1, source_target_pairs={{0,8},{8,0},{1,9},{9,1},{2,10},{10,2},{3,11},{11,3},{4,12},{12,4},... | collective-permute-start | bytes 5505032 | tf_op jit(solution)/shard_map/ppermute | solution.py:178
  8.5 2.1 %copy-start.4 = (f32[2]{0:T(128)S(1)}, f32[2]{0:T(128)}, u32[]{:S(2)}) copy-start(f32[2]{0:T(128)} %constant.28.clone) | copy-start | bytes 28
  10.7 11.6 %collective-permute-start.1 = (f32[5]{0:T(128)S(1)}, f32[5]{0:T(128)S(1)}, u32[]{:S(2)}, u32[]{:S(2)}) collective-permute-start(f32[5]{0:T(128)S(1)} %fusion.3), channel_id=1, source_target_pairs={{8,108},{9,109},{10,110},{11,111},{12,104},{13,105},{14,106},{15,1... | collective-permute-start | bytes 68 | tf_op jit(solution)/shard_map/ppermute | solution.py:229
  22.3 8.2 %collective-permute-start.2 = (f32[5]{0:T(128)S(1)}, f32[5]{0:T(128)S(1)}, u32[]{:S(2)}, u32[]{:S(2)}) collective-permute-start(f32[5]{0:T(128)S(1)} %collective-permute-done.1), channel_id=1, source_target_pairs={{8,44},{9,45},{10,46},{11,47},{12,40},{13,41},{14,42},{15,43},{24,... | collective-permute-start | bytes 68 | tf_op jit(solution)/shard_map/ppermute | solution.py:229
  31.7 41.6 %copy-start = (f32[8,28672]{1,0:T(8,128)S(1)}, f32[8,28672]{1,0:T(8,128)}, u32[]{:S(2)}) copy-start(f32[8,28672]{1,0:T(8,128)} %master_ref.1) | copy-start | bytes 2752516
  31.7 41.6 %copy-start.1 = (f32[8,28672]{1,0:T(8,128)S(1)}, f32[8,28672]{1,0:T(8,128)}, u32[]{:S(2)}) copy-start(f32[8,28672]{1,0:T(8,128)} %first_ref.1) | copy-start | bytes 2752516
  31.7 41.6 %copy-start.2 = (f32[8,28672]{1,0:T(8,128)S(1)}, f32[8,28672]{1,0:T(8,128)}, u32[]{:S(2)}) copy-start(f32[8,28672]{1,0:T(8,128)} %second_ref.1) | copy-start | bytes 2752516
  115.8 4.5 %collective-permute-start.5 = (bf16[5,8,8,3584]{3,2,1,0:T(8,128)(2,1)S(1)}, bf16[5,8,8,3584]{3,2,1,0:T(8,128)(2,1)S(1)}, u32[]{:S(2)}, u32[]{:S(2)}) collective-permute-start(bf16[5,8,8,3584]{3,2,1,0:T(8,128)(2,1)S(1)} %slice.14), channel_id=1, source_target_pairs={{0,8},{8,0},{1,9},{9,1},{2,10},{10,2},{3,11},{11,3},{4,12},{12,4},... | collective-permute-start | bytes 6881288 | tf_op jit(solution)/shard_map/ppermute | solution.py:178
  116.1 6.3 %collective-permute-start.4 = (bf16[3,8,8,3584]{3,2,1,0:T(8,128)(2,1)S(1)}, bf16[3,8,8,3584]{3,2,1,0:T(8,128)(2,1)S(1)}, u32[]{:S(2)}, u32[]{:S(2)}) collective-permute-start(bf16[3,8,8,3584]{3,2,1,0:T(8,128)(2,1)S(1)} %slice.13), channel_id=1, source_target_pairs={{0,8},{8,0},{1,9},{9,1},{2,10},{10,2},{3,11},{11,3},{4,12},{12,4},... | collective-permute-start | bytes 4128776 | tf_op jit(solution)/shard_map/ppermute | solution.py:178

commit v6 on v5

--- a/solution.py
+++ b/solution.py
@@ -203,7 +203,7 @@
     )(*wait, in_vmem(a), in_vmem(b), *more)[0]
 
 
-TURN = (("z_hi", "x", "y"), ("x", "y"))
+TURN = (("z_hi", "x", "y"), ("x", "y", "z_lo"))
 MESH = ("z_hi", "x", "core", "y", "z_lo")
 SIZES = {"z_hi": Z, "x": X, "core": 2, "y": Y, "z_lo": 2}
 

time: 124 us -> 123 us (level)
  blocking collectives: 81.9 us -> 79.6 us
  starting transfers between devices: 19.3 us -> 20.6 us
    all_to_all x1, blocking collectives: 40.3 us -> 36.2 us  [local(): lax.all_to_all(spread.reshape(T * chips, own, columns), GROUP, split_axis...]
    all_to_all x1, blocking collectives: 41.6 us -> 43.4 us  [local(): lax.all_to_all(pieces.reshape(T * chips, own, columns), GROUP, split_axis...]
    ppermute x2, starting transfers between devices: 17 us -> 18.4 us  [after_turn(): token = lax.ppermute(token, MESH, pairs)]
where the time goes in v6:
time: 123 us
  blocking collectives  79.6 us (65%)
  starting transfers between devices  20.6 us (17%)
  Pallas kernels  18.3 us (15%)
  waiting for transfers between devices  2.22 us (2%)
  between operations  1.51 us (1%)
    all_to_all x1, blocking collectives, local(): lax.all_to_all(pieces.reshape(T * chips, own, columns), GROUP, split_axis...  43.4 us
    all_to_all x1, blocking collectives, local(): lax.all_to_all(spread.reshape(T * chips, own, columns), GROUP, split_axis...  36.2 us
    ppermute x2, starting transfers between devices, after_turn(): token = lax.ppermute(token, MESH, pairs)  18.4 us
    pallas_call x2, Pallas kernels, split(): copying(body, len(parts), out, 1, moved=moved, name=name)  5.5 us
    pallas_call x2, Pallas kernels, place_other(): return call(ids, in_vmem(pieces), into)  3.6 us
    pallas_call x1, Pallas kernels, place_own(): return call(ids, *[in_vmem(a) for a in (pieces, *states)])  3.34 us
  transfers between devices with their start and end apart: 6, of which 3 were waited for; matrix products, arithmetic and copies ran while one was open for 0% of the time, Pallas kernels for 9%

profile of v6, /device:TPU:1, one launch (start us, length us, event | category | flops | bytes accessed | tf_op | source)
XLA Modules:
  0.0 122.7 jit_solution(9507162174642679288)
XLA Ops:
  0.6 0.1 stack.23.ids_ref
  0.7 0.0 slice-start
  0.7 0.0 slice-start.1
  0.7 2.3 %split_first.1 = bf16[4,64,3584]{2,1,0:T(8,128)(2,1)S(1)} custom-call(s32[5]{0:T(128)S(1)} %stack.23.ids_ref, bf16[8,2,64,3584]{3,2,1,0:T(8,128)(2,1)} %bitcast.25), custom_call_target="tpu_custom_call" | custom-call | bytes 3670016 | tf_op jit(solution)/shard_map/split_first/pallas_call | solution.py:75
  3.1 0.0 copy-start.3
  3.1 1.5 %collective-permute-start = (bf16[4,64,3584]{2,1,0:T(8,128)(2,1)S(1)}, bf16[4,64,3584]{2,1,0:T(8,128)(2,1)S(1)}, u32[]{:S(2)}, u32[]{:S(2)}) collective-permute-start(bf16[4,64,3584]{2,1,0:T(8,128)(2,1)S(1)} %split_first.1), channel_id=1, source_target_pairs={{0,8},{8,0},{1,9},{9,1},{2,10},{10,2},{3,11},{11,3},{4,12},{12,4},... | collective-permute-start | bytes 5505032 | tf_op jit(solution)/shard_map/ppermute | solution.py:178
  4.6 3.2 %split_rest.1 = (bf16[4,64,3584]{2,1,0:T(8,128)(2,1)S(1)}, bf16[4,64,3584]{2,1,0:T(8,128)(2,1)S(1)}, bf16[4,64,3584]{2,1,0:T(8,128)(2,1)S(1)}) custom-call(s32[5]{0:T(128)S(1)} %stack.23.ids_ref, bf16[8,2,64,3584]{3,2,1,0:T(8,128)(2,1)} %bitcast.26), custom_call_target="tpu_custom_call" | custom-call | bytes 11010048 | tf_op jit(solution)/shard_map/split_rest/pallas_call | solution.py:75
  7.8 0.1 collective-permute-start.3
  8.5 0.0 slice-done
  8.5 0.0 slice-done.1
  8.5 0.0 copy-done.3
  8.5 0.0 copy-start.4
  8.6 2.0 %noise_sum.1.noise_ref = f32[8,28672]{1,0:T(8,128)S(1)} custom-call(s32[16]{0:T(128)S(1)} %copy-done.3, s32[1]{0:T(128)S(6)} %copy.18.step_ref, bf16[16,8,28672]{2,1,0:T(8,128)(2,1)S(1)} %bitcast.22), custom_call_target="tpu_custom_call" | custom-call | flops 7340032 | bytes 7340032 | tf_op jit(solution)/shard_map/noise_sum/pallas_call | solution.py:121
  10.6 0.0 copy-done.4
  10.6 0.0 collective-permute-done.refs_1_
  10.7 10.7 %collective-permute-start.1 = (f32[5]{0:T(128)S(1)}, f32[5]{0:T(128)S(1)}, u32[]{:S(2)}, u32[]{:S(2)}) collective-permute-start(f32[5]{0:T(128)S(1)} %fusion.3), channel_id=1, source_target_pairs={{8,108},{9,109},{10,110},{11,111},{12,104},{13,105},{14,106},{15,1... | collective-permute-start | bytes 68 | tf_op jit(solution)/shard_map/ppermute | solution.py:229
  21.3 0.6 plus.2.refs_3_
  22.0 0.3 collective-permute-done.1
  22.3 7.7 %collective-permute-start.2 = (f32[5]{0:T(128)S(1)}, f32[5]{0:T(128)S(1)}, u32[]{:S(2)}, u32[]{:S(2)}) collective-permute-start(f32[5]{0:T(128)S(1)} %collective-permute-done.1), channel_id=1, source_target_pairs={{8,45},{9,44},{10,47},{11,46},{12,41},{13,40},{14,43},{15,42},{24,... | collective-permute-start | bytes 68 | tf_op jit(solution)/shard_map/ppermute | solution.py:229
  30.0 1.5 %collective-permute-done.2 = f32[5]{0:T(128)S(1)} collective-permute-done((f32[5]{0:T(128)S(1)}, f32[5]{0:T(128)S(1)}, u32[]{:S(2)}, u32[]{:S(2)}) %collective-permute-start.2) | collective-permute-done | bytes 52 | tf_op jit(solution)/shard_map/ppermute | solution.py:229
  31.5 0.0 collective-permute-done.3.refs_2_
  31.5 1.2 plus.3
  32.7 0.0 copy-start
  32.7 0.0 copy-start.1
  32.7 0.0 copy-start.2
  32.7 43.4 %all_to_all.10 = bf16[64,8,3584]{2,1,0:T(8,128)(2,1)S(1)} all-to-all(bf16[64,8,3584]{2,1,0:T(8,128)(2,1)S(1)} %bitcast.16), channel_id=1, replica_groups=mesh['z_hi'=2,'x'=4,'core'=2,'y'=4,'z_lo'=2] {'y','z_lo','z_hi','x'}, dimensions={0} | all-to-all | bytes 7340032 | tf_op jit(solution)/shard_map/all_to_all | solution.py:256
  76.1 0.0 copy-done
  76.1 0.0 copy-done.1
  76.1 0.0 copy-done.2
  76.2 2.1 %adam_step.1 = (f32[8,28672]{1,0:T(8,128)S(1)}, f32[8,28672]{1,0:T(8,128)S(1)}, f32[8,28672]{1,0:T(8,128)S(1)}, bf16[8,8,8,3584]{3,2,1,0:T(8,128)(2,1)S(1)}) custom-call(f32[2]{0:T(128)S(1)} %power_subtract_fusion.correct_ref, bf16[8,8,8,3584]{3,2,1,0:T(8,128)(2,1)S(1)} %bitcast.20, f32[8,28672]{1,0:T(8,128)S(1)} %noise_sum.1.noise_ref, ...), custom_call_target="tpu_custom_call" | custom-call | tf_op jit(solution)/shard_map/adam_step/pallas_call | solution.py:166
  78.2 36.2 %all_to_all.11 = bf16[64,8,3584]{2,1,0:T(8,128)(2,1)S(1)} all-to-all(bf16[64,8,3584]{2,1,0:T(8,128)(2,1)S(1)} %bitcast.23), channel_id=1, replica_groups=mesh['z_hi'=2,'x'=4,'core'=2,'y'=4,'z_lo'=2] {'y','z_lo','z_hi','x'}, dimensions={0} | all-to-all | bytes 7340032 | tf_op jit(solution)/shard_map/all_to_all | solution.py:261
  114.4 0.2 slice.14
  114.6 0.1 collective-permute-start.5
  114.7 0.1 slice.13
  114.8 0.6 collective-permute-start.4
  115.4 3.3 %place_own.1 = (bf16[8,2,8,8,3584]{4,3,2,1,0:T(8,128)(2,1)}, f32[8,28672]{1,0:T(8,128)}, f32[8,28672]{1,0:T(8,128)}, f32[8,28672]{1,0:T(8,128)}) custom-call(s32[5]{0:T(128)S(1)} %stack.23.ids_ref, bf16[8,8,8,3584]{3,2,1,0:T(8,128)(2,1)S(1)} %bitcast.19, f32[8,28672]{1,0:T(8,128)S(1)} %get-tuple-element.33.refs_1_, ...), custom_call_target="tpu_custom_call" | custom-call | bytes 12845056 | tf_op jit(solution)/shard_map/place_own/pallas_call | solution.py:88
  118.7 0.4 collective-permute-done.5.refs_0_
  119.1 2.0 %place_early.1.refs_1_ = bf16[8,2,8,8,3584]{4,3,2,1,0:T(8,128)(2,1)} custom-call(s32[5]{0:T(128)S(1)} %stack.23.ids_ref, bf16[5,8,8,3584]{3,2,1,0:T(8,128)(2,1)S(1)} %collective-permute-done.5.refs_0_, bf16[8,2,8,8,3584]{4,3,2,1,0:T(8,128)(2,1)} %get-tuple-element.39.refs_1_), custom_call_target="tpu_custom_call", output_to_operand_aliasing={{}: (2, {})} | custom-call | bytes 4587520 | tf_op jit(solution)/shard_map/place_early/pallas_call | solution.py:98
  121.1 0.0 collective-permute-done.4.refs_0_
  121.1 1.6 %place_late.1 = bf16[8,2,8,8,3584]{4,3,2,1,0:T(8,128)(2,1)} custom-call(s32[5]{0:T(128)S(1)} %stack.23.ids_ref, bf16[3,8,8,3584]{3,2,1,0:T(8,128)(2,1)S(1)} %collective-permute-done.4.refs_0_, bf16[8,2,8,8,3584]{4,3,2,1,0:T(8,128)(2,1)} %place_early.1.refs_1_), custom_call_target="tpu_custom_call", output_to_operand_aliasing={{}: (2, {})} | custom-call | bytes 2752512 | tf_op jit(solution)/shard_map/place_late/pallas_call | solution.py:98
  (4 shorter events, 0.0 us)
Async XLA Ops:
  0.7 7.8 %slice-start = ((s8[7340032]{0:T(1024)(128)(4,1)}), s8[4194304]{0:T(1024)(128)(4,1)S(1)}, s32[]{:S(2)}) async-start(s8[7340032]{0:T(1024)(128)(4,1)} %bitcast.21), calls=%async_computation.2 | async-start | bytes 8388608
  0.7 7.8 %slice-start.1 = ((s8[7340032]{0:T(1024)(128)(4,1)}), s8[3145728]{0:T(1024)(128)(4,1)S(1)}, s32[]{:S(2)}) async-start(s8[7340032]{0:T(1024)(128)(4,1)} %bitcast.21), calls=%async_computation.3 | async-start | bytes 6291456
  3.1 5.5 %copy-start.3 = (s32[16]{0:T(128)S(1)}, s32[16]{0:T(128)}, u32[]{:S(2)}) copy-start(s32[16]{0:T(128)} %coeffs_ref.1) | copy-start | bytes 196
  3.1 7.6 %collective-permute-start = (bf16[4,64,3584]{2,1,0:T(8,128)(2,1)S(1)}, bf16[4,64,3584]{2,1,0:T(8,128)(2,1)S(1)}, u32[]{:S(2)}, u32[]{:S(2)}) collective-permute-start(bf16[4,64,3584]{2,1,0:T(8,128)(2,1)S(1)} %split_first.1), channel_id=1, source_target_pairs={{0,8},{8,0},{1,9},{9,1},{2,10},{10,2},{3,11},{11,3},{4,12},{12,4},... | collective-permute-start | bytes 5505032 | tf_op jit(solution)/shard_map/ppermute | solution.py:178
  7.8 23.8 %collective-permute-start.3 = (bf16[4,64,3584]{2,1,0:T(8,128)(2,1)S(1)}, bf16[4,64,3584]{2,1,0:T(8,128)(2,1)S(1)}, u32[]{:S(2)}, u32[]{:S(2)}) collective-permute-start(bf16[4,64,3584]{2,1,0:T(8,128)(2,1)S(1)} %get-tuple-element.23), channel_id=1, source_target_pairs={{0,8},{8,0},{1,9},{9,1},{2,10},{10,2},{3,11},{11,3},{4,12},{12,4},... | collective-permute-start | bytes 5505032 | tf_op jit(solution)/shard_map/ppermute | solution.py:178
  8.5 2.1 %copy-start.4 = (f32[2]{0:T(128)S(1)}, f32[2]{0:T(128)}, u32[]{:S(2)}) copy-start(f32[2]{0:T(128)} %constant.28.clone) | copy-start | bytes 28
  10.7 11.6 %collective-permute-start.1 = (f32[5]{0:T(128)S(1)}, f32[5]{0:T(128)S(1)}, u32[]{:S(2)}, u32[]{:S(2)}) collective-permute-start(f32[5]{0:T(128)S(1)} %fusion.3), channel_id=1, source_target_pairs={{8,108},{9,109},{10,110},{11,111},{12,104},{13,105},{14,106},{15,1... | collective-permute-start | bytes 68 | tf_op jit(solution)/shard_map/ppermute | solution.py:229
  22.3 9.2 %collective-permute-start.2 = (f32[5]{0:T(128)S(1)}, f32[5]{0:T(128)S(1)}, u32[]{:S(2)}, u32[]{:S(2)}) collective-permute-start(f32[5]{0:T(128)S(1)} %collective-permute-done.1), channel_id=1, source_target_pairs={{8,45},{9,44},{10,47},{11,46},{12,41},{13,40},{14,43},{15,42},{24,... | collective-permute-start | bytes 68 | tf_op jit(solution)/shard_map/ppermute | solution.py:229
  32.7 43.5 %copy-start = (f32[8,28672]{1,0:T(8,128)S(1)}, f32[8,28672]{1,0:T(8,128)}, u32[]{:S(2)}) copy-start(f32[8,28672]{1,0:T(8,128)} %master_ref.1) | copy-start | bytes 2752516
  32.7 43.4 %copy-start.1 = (f32[8,28672]{1,0:T(8,128)S(1)}, f32[8,28672]{1,0:T(8,128)}, u32[]{:S(2)}) copy-start(f32[8,28672]{1,0:T(8,128)} %first_ref.1) | copy-start | bytes 2752516
  32.7 43.4 %copy-start.2 = (f32[8,28672]{1,0:T(8,128)S(1)}, f32[8,28672]{1,0:T(8,128)}, u32[]{:S(2)}) copy-start(f32[8,28672]{1,0:T(8,128)} %second_ref.1) | copy-start | bytes 2752516
  114.6 4.5 %collective-permute-start.5 = (bf16[5,8,8,3584]{3,2,1,0:T(8,128)(2,1)S(1)}, bf16[5,8,8,3584]{3,2,1,0:T(8,128)(2,1)S(1)}, u32[]{:S(2)}, u32[]{:S(2)}) collective-permute-start(bf16[5,8,8,3584]{3,2,1,0:T(8,128)(2,1)S(1)} %slice.14), channel_id=1, source_target_pairs={{0,8},{8,0},{1,9},{9,1},{2,10},{10,2},{3,11},{11,3},{4,12},{12,4},... | collective-permute-start | bytes 6881288 | tf_op jit(solution)/shard_map/ppermute | solution.py:178
  114.8 6.3 %collective-permute-start.4 = (bf16[3,8,8,3584]{3,2,1,0:T(8,128)(2,1)S(1)}, bf16[3,8,8,3584]{3,2,1,0:T(8,128)(2,1)S(1)}, u32[]{:S(2)}, u32[]{:S(2)}) collective-permute-start(bf16[3,8,8,3584]{3,2,1,0:T(8,128)(2,1)S(1)} %slice.13), channel_id=1, source_target_pairs={{0,8},{8,0},{1,9},{9,1},{2,10},{10,2},{3,11},{11,3},{4,12},{12,4},... | collective-permute-start | bytes 4128776 | tf_op jit(solution)/shard_map/ppermute | solution.py:178

commit v7 on v6

--- a/solution.py
+++ b/solution.py
@@ -12,7 +12,7 @@
 DP = ("z_hi", "x", "core")
 TENSOR = ("y", "z_lo")
 Z, X, Y, T = 2, 4, 4, 8
-EARLY = 5
+EARLY = 6
 VMEM_BYTES = 16 * 1024 * 1024
 SMALL = 1024 * 1024
 SMEM = pl.BlockSpec(memory_space=pltpu.SMEM)
@@ -195,7 +195,7 @@
         functools.partial(plus_kernel, len(wait)),
         out_shape=[pltpu.VMEM((T, chips, rows // T, columns), BF16)],
         grid=(n,),
-        in_specs=[SMEM] * len(wait) + [block, block] + [ANY] * len(more),
+        in_specs=[ANY] * len(wait) + [block, block] + [ANY] * len(more),
         out_specs=[pl.BlockSpec((T, 1, rows // T, columns), lambda i: (0, first + i, 0, 0))],
         input_output_aliases={len(wait) + 2: 0} if more else {},
         compiler_params=pltpu.CompilerParams(vmem_limit_bytes=VMEM_BYTES),

time: 123 us -> 123 us (level)
    all_to_all x1, blocking collectives: 43.4 us -> 40.6 us  [local(): lax.all_to_all(pieces.reshape(T * chips, own, columns), GROUP, split_axis...]
    all_to_all x1, blocking collectives: 36.2 us -> 38.8 us  [local(): lax.all_to_all(spread.reshape(T * chips, own, columns), GROUP, split_axis...]
where the time goes in v7:
time: 123 us
  blocking collectives  79.4 us (65%)
  starting transfers between devices  20.6 us (17%)
  Pallas kernels  17.8 us (14%)
  waiting for transfers between devices  2.97 us (2%)
  between operations  1.51 us (1%)
    all_to_all x1, blocking collectives, local(): lax.all_to_all(pieces.reshape(T * chips, own, columns), GROUP, split_axis...  40.6 us
    all_to_all x1, blocking collectives, local(): lax.all_to_all(spread.reshape(T * chips, own, columns), GROUP, split_axis...  38.8 us
    ppermute x2, starting transfers between devices, after_turn(): token = lax.ppermute(token, MESH, pairs)  18.4 us
    pallas_call x2, Pallas kernels, split(): copying(body, len(parts), out, 1, moved=moved, name=name)  5.5 us
    pallas_call x2, Pallas kernels, place_other(): return call(ids, in_vmem(pieces), into)  3.6 us
    pallas_call x1, Pallas kernels, place_own(): return call(ids, *[in_vmem(a) for a in (pieces, *states)])  3.34 us
  transfers between devices with their start and end apart: 6, of which 3 were waited for; matrix products, arithmetic and copies ran while one was open for 0% of the time, Pallas kernels for 9%

profile of v7, /device:TPU:1, one launch (start us, length us, event | category | flops | bytes accessed | tf_op | source)
XLA Modules:
  0.0 122.8 jit_solution(8502994623962547823)
XLA Ops:
  0.6 0.1 stack.23.ids_ref
  0.7 0.0 slice-start
  0.7 0.0 slice-start.1
  0.7 2.3 %split_first.1 = bf16[4,64,3584]{2,1,0:T(8,128)(2,1)S(1)} custom-call(s32[5]{0:T(128)S(1)} %stack.23.ids_ref, bf16[8,2,64,3584]{3,2,1,0:T(8,128)(2,1)} %bitcast.25), custom_call_target="tpu_custom_call" | custom-call | bytes 3670016 | tf_op jit(solution)/shard_map/split_first/pallas_call | solution.py:75
  3.1 0.0 copy-start.3
  3.1 1.5 %collective-permute-start = (bf16[4,64,3584]{2,1,0:T(8,128)(2,1)S(1)}, bf16[4,64,3584]{2,1,0:T(8,128)(2,1)S(1)}, u32[]{:S(2)}, u32[]{:S(2)}) collective-permute-start(bf16[4,64,3584]{2,1,0:T(8,128)(2,1)S(1)} %split_first.1), channel_id=1, source_target_pairs={{0,8},{8,0},{1,9},{9,1},{2,10},{10,2},{3,11},{11,3},{4,12},{12,4},... | collective-permute-start | bytes 5505032 | tf_op jit(solution)/shard_map/ppermute | solution.py:178
  4.6 3.2 %split_rest.1 = (bf16[4,64,3584]{2,1,0:T(8,128)(2,1)S(1)}, bf16[4,64,3584]{2,1,0:T(8,128)(2,1)S(1)}, bf16[4,64,3584]{2,1,0:T(8,128)(2,1)S(1)}) custom-call(s32[5]{0:T(128)S(1)} %stack.23.ids_ref, bf16[8,2,64,3584]{3,2,1,0:T(8,128)(2,1)} %bitcast.26), custom_call_target="tpu_custom_call" | custom-call | bytes 11010048 | tf_op jit(solution)/shard_map/split_rest/pallas_call | solution.py:75
  7.8 0.1 collective-permute-start.3
  8.5 0.0 slice-done
  8.5 0.0 slice-done.1
  8.5 0.0 copy-done.3
  8.5 0.0 copy-start.4
  8.6 2.0 %noise_sum.1.noise_ref = f32[8,28672]{1,0:T(8,128)S(1)} custom-call(s32[16]{0:T(128)S(1)} %copy-done.3, s32[1]{0:T(128)S(6)} %copy.18.step_ref, bf16[16,8,28672]{2,1,0:T(8,128)(2,1)S(1)} %bitcast.22), custom_call_target="tpu_custom_call" | custom-call | flops 7340032 | bytes 7340032 | tf_op jit(solution)/shard_map/noise_sum/pallas_call | solution.py:121
  10.6 0.0 copy-done.4
  10.6 0.0 collective-permute-done.refs_1_
  10.7 10.7 %collective-permute-start.1 = (f32[5]{0:T(128)S(1)}, f32[5]{0:T(128)S(1)}, u32[]{:S(2)}, u32[]{:S(2)}) collective-permute-start(f32[5]{0:T(128)S(1)} %fusion.3), channel_id=1, source_target_pairs={{8,108},{9,109},{10,110},{11,111},{12,104},{13,105},{14,106},{15,1... | collective-permute-start | bytes 68 | tf_op jit(solution)/shard_map/ppermute | solution.py:229
  21.3 0.6 plus.2.refs_3_
  22.0 0.3 collective-permute-done.1
  22.3 7.7 %collective-permute-start.2 = (f32[5]{0:T(128)S(1)}, f32[5]{0:T(128)S(1)}, u32[]{:S(2)}, u32[]{:S(2)}) collective-permute-start(f32[5]{0:T(128)S(1)} %collective-permute-done.1), channel_id=1, source_target_pairs={{8,45},{9,44},{10,47},{11,46},{12,41},{13,40},{14,43},{15,42},{24,... | collective-permute-start | bytes 68 | tf_op jit(solution)/shard_map/ppermute | solution.py:229
  30.0 1.6 %collective-permute-done.2 = f32[5]{0:T(128)S(1)} collective-permute-done((f32[5]{0:T(128)S(1)}, f32[5]{0:T(128)S(1)}, u32[]{:S(2)}, u32[]{:S(2)}) %collective-permute-start.2) | collective-permute-done | bytes 52 | tf_op jit(solution)/shard_map/ppermute | solution.py:229
  31.6 0.0 collective-permute-done.3.refs_2_
  31.6 0.6 plus.3
  32.2 0.0 copy-start
  32.2 0.0 copy-start.1
  32.2 0.0 copy-start.2
  32.2 40.6 %all_to_all.10 = bf16[64,8,3584]{2,1,0:T(8,128)(2,1)S(1)} all-to-all(bf16[64,8,3584]{2,1,0:T(8,128)(2,1)S(1)} %bitcast.16), channel_id=1, replica_groups=mesh['z_hi'=2,'x'=4,'core'=2,'y'=4,'z_lo'=2] {'y','z_lo','z_hi','x'}, dimensions={0} | all-to-all | bytes 7340032 | tf_op jit(solution)/shard_map/all_to_all | solution.py:256
  72.8 0.0 copy-done
  72.8 0.0 copy-done.1
  72.8 0.0 copy-done.2
  72.8 2.1 %adam_step.1 = (f32[8,28672]{1,0:T(8,128)S(1)}, f32[8,28672]{1,0:T(8,128)S(1)}, f32[8,28672]{1,0:T(8,128)S(1)}, bf16[8,8,8,3584]{3,2,1,0:T(8,128)(2,1)S(1)}) custom-call(f32[2]{0:T(128)S(1)} %power_subtract_fusion.correct_ref, bf16[8,8,8,3584]{3,2,1,0:T(8,128)(2,1)S(1)} %bitcast.20, f32[8,28672]{1,0:T(8,128)S(1)} %noise_sum.1.noise_ref, ...), custom_call_target="tpu_custom_call" | custom-call | tf_op jit(solution)/shard_map/adam_step/pallas_call | solution.py:166
  74.9 38.8 %all_to_all.11 = bf16[64,8,3584]{2,1,0:T(8,128)(2,1)S(1)} all-to-all(bf16[64,8,3584]{2,1,0:T(8,128)(2,1)S(1)} %bitcast.23), channel_id=1, replica_groups=mesh['z_hi'=2,'x'=4,'core'=2,'y'=4,'z_lo'=2] {'y','z_lo','z_hi','x'}, dimensions={0} | all-to-all | bytes 7340032 | tf_op jit(solution)/shard_map/all_to_all | solution.py:261
  113.7 0.2 slice.14
  114.0 0.1 collective-permute-start.5
  114.1 0.1 slice.13
  114.1 0.6 collective-permute-start.4
  114.7 3.3 %place_own.1 = (bf16[8,2,8,8,3584]{4,3,2,1,0:T(8,128)(2,1)}, f32[8,28672]{1,0:T(8,128)}, f32[8,28672]{1,0:T(8,128)}, f32[8,28672]{1,0:T(8,128)}) custom-call(s32[5]{0:T(128)S(1)} %stack.23.ids_ref, bf16[8,8,8,3584]{3,2,1,0:T(8,128)(2,1)S(1)} %bitcast.19, f32[8,28672]{1,0:T(8,128)S(1)} %get-tuple-element.33.refs_1_, ...), custom_call_target="tpu_custom_call" | custom-call | bytes 12845056 | tf_op jit(solution)/shard_map/place_own/pallas_call | solution.py:88
  118.1 1.1 collective-permute-done.5.refs_0_
  119.2 2.1 %place_early.1.refs_1_ = bf16[8,2,8,8,3584]{4,3,2,1,0:T(8,128)(2,1)} custom-call(s32[5]{0:T(128)S(1)} %stack.23.ids_ref, bf16[6,8,8,3584]{3,2,1,0:T(8,128)(2,1)S(1)} %collective-permute-done.5.refs_0_, bf16[8,2,8,8,3584]{4,3,2,1,0:T(8,128)(2,1)} %get-tuple-element.39.refs_1_), custom_call_target="tpu_custom_call", output_to_operand_aliasing={{}: (2, {})} | custom-call | bytes 5505024 | tf_op jit(solution)/shard_map/place_early/pallas_call | solution.py:98
  121.3 0.0 collective-permute-done.4.refs_0_
  121.3 1.5 %place_late.1 = bf16[8,2,8,8,3584]{4,3,2,1,0:T(8,128)(2,1)} custom-call(s32[5]{0:T(128)S(1)} %stack.23.ids_ref, bf16[2,8,8,3584]{3,2,1,0:T(8,128)(2,1)S(1)} %collective-permute-done.4.refs_0_, bf16[8,2,8,8,3584]{4,3,2,1,0:T(8,128)(2,1)} %place_early.1.refs_1_), custom_call_target="tpu_custom_call", output_to_operand_aliasing={{}: (2, {})} | custom-call | bytes 1835008 | tf_op jit(solution)/shard_map/place_late/pallas_call | solution.py:98
  (4 shorter events, 0.0 us)
Async XLA Ops:
  0.7 7.8 %slice-start = ((s8[7340032]{0:T(1024)(128)(4,1)}), s8[4194304]{0:T(1024)(128)(4,1)S(1)}, s32[]{:S(2)}) async-start(s8[7340032]{0:T(1024)(128)(4,1)} %bitcast.21), calls=%async_computation.2 | async-start | bytes 8388608
  0.7 7.8 %slice-start.1 = ((s8[7340032]{0:T(1024)(128)(4,1)}), s8[3145728]{0:T(1024)(128)(4,1)S(1)}, s32[]{:S(2)}) async-start(s8[7340032]{0:T(1024)(128)(4,1)} %bitcast.21), calls=%async_computation.3 | async-start | bytes 6291456
  3.1 5.5 %copy-start.3 = (s32[16]{0:T(128)S(1)}, s32[16]{0:T(128)}, u32[]{:S(2)}) copy-start(s32[16]{0:T(128)} %coeffs_ref.1) | copy-start | bytes 196
  3.1 7.6 %collective-permute-start = (bf16[4,64,3584]{2,1,0:T(8,128)(2,1)S(1)}, bf16[4,64,3584]{2,1,0:T(8,128)(2,1)S(1)}, u32[]{:S(2)}, u32[]{:S(2)}) collective-permute-start(bf16[4,64,3584]{2,1,0:T(8,128)(2,1)S(1)} %split_first.1), channel_id=1, source_target_pairs={{0,8},{8,0},{1,9},{9,1},{2,10},{10,2},{3,11},{11,3},{4,12},{12,4},... | collective-permute-start | bytes 5505032 | tf_op jit(solution)/shard_map/ppermute | solution.py:178
  7.8 23.8 %collective-permute-start.3 = (bf16[4,64,3584]{2,1,0:T(8,128)(2,1)S(1)}, bf16[4,64,3584]{2,1,0:T(8,128)(2,1)S(1)}, u32[]{:S(2)}, u32[]{:S(2)}) collective-permute-start(bf16[4,64,3584]{2,1,0:T(8,128)(2,1)S(1)} %get-tuple-element.23), channel_id=1, source_target_pairs={{0,8},{8,0},{1,9},{9,1},{2,10},{10,2},{3,11},{11,3},{4,12},{12,4},... | collective-permute-start | bytes 5505032 | tf_op jit(solution)/shard_map/ppermute | solution.py:178
  8.5 2.1 %copy-start.4 = (f32[2]{0:T(128)S(1)}, f32[2]{0:T(128)}, u32[]{:S(2)}) copy-start(f32[2]{0:T(128)} %constant.28.clone) | copy-start | bytes 28
  10.7 11.6 %collective-permute-start.1 = (f32[5]{0:T(128)S(1)}, f32[5]{0:T(128)S(1)}, u32[]{:S(2)}, u32[]{:S(2)}) collective-permute-start(f32[5]{0:T(128)S(1)} %fusion.3), channel_id=1, source_target_pairs={{8,108},{9,109},{10,110},{11,111},{12,104},{13,105},{14,106},{15,1... | collective-permute-start | bytes 68 | tf_op jit(solution)/shard_map/ppermute | solution.py:229
  22.3 9.3 %collective-permute-start.2 = (f32[5]{0:T(128)S(1)}, f32[5]{0:T(128)S(1)}, u32[]{:S(2)}, u32[]{:S(2)}) collective-permute-start(f32[5]{0:T(128)S(1)} %collective-permute-done.1), channel_id=1, source_target_pairs={{8,45},{9,44},{10,47},{11,46},{12,41},{13,40},{14,43},{15,42},{24,... | collective-permute-start | bytes 68 | tf_op jit(solution)/shard_map/ppermute | solution.py:229
  32.2 40.6 %copy-start = (f32[8,28672]{1,0:T(8,128)S(1)}, f32[8,28672]{1,0:T(8,128)}, u32[]{:S(2)}) copy-start(f32[8,28672]{1,0:T(8,128)} %master_ref.1) | copy-start | bytes 2752516
  32.2 40.6 %copy-start.1 = (f32[8,28672]{1,0:T(8,128)S(1)}, f32[8,28672]{1,0:T(8,128)}, u32[]{:S(2)}) copy-start(f32[8,28672]{1,0:T(8,128)} %first_ref.1) | copy-start | bytes 2752516
  32.2 40.6 %copy-start.2 = (f32[8,28672]{1,0:T(8,128)S(1)}, f32[8,28672]{1,0:T(8,128)}, u32[]{:S(2)}) copy-start(f32[8,28672]{1,0:T(8,128)} %second_ref.1) | copy-start | bytes 2752516
  114.0 5.2 %collective-permute-start.5 = (bf16[6,8,8,3584]{3,2,1,0:T(8,128)(2,1)S(1)}, bf16[6,8,8,3584]{3,2,1,0:T(8,128)(2,1)S(1)}, u32[]{:S(2)}, u32[]{:S(2)}) collective-permute-start(bf16[6,8,8,3584]{3,2,1,0:T(8,128)(2,1)S(1)} %slice.14), channel_id=1, source_target_pairs={{0,8},{8,0},{1,9},{9,1},{2,10},{10,2},{3,11},{11,3},{4,12},{12,4},... | collective-permute-start | bytes 8257544 | tf_op jit(solution)/shard_map/ppermute | solution.py:178
  114.1 7.1 %collective-permute-start.4 = (bf16[2,8,8,3584]{3,2,1,0:T(8,128)(2,1)S(1)}, bf16[2,8,8,3584]{3,2,1,0:T(8,128)(2,1)S(1)}, u32[]{:S(2)}, u32[]{:S(2)}) collective-permute-start(bf16[2,8,8,3584]{3,2,1,0:T(8,128)(2,1)S(1)} %slice.13), channel_id=1, source_target_pairs={{0,8},{8,0},{1,9},{9,1},{2,10},{10,2},{3,11},{11,3},{4,12},{12,4},... | collective-permute-start | bytes 2752520 | tf_op jit(solution)/shard_map/ppermute | solution.py:178
